TPU v7x, 32 devices: a whole 2x2x4 slice. The times are simulated.
32 devices in a mesh: seq: 8 (over z, y), fsdp: 4 (over x, core).
Axes of the slice: x: 2, y: 2, z: 4, core: 2. Of those that a mesh axis runs over, the one named last changes fastest.
Arguments:
- inputs: bfloat16 [4, 1024, 2560], P('fsdp', 'seq'), may hold values from -6 to 6
- resets: int32 [4, 1024], P('fsdp', 'seq'), may hold values from 0 to 1, as said below
- cotangent: bfloat16 [4, 1024, 2560], P('fsdp', 'seq'), may hold values from -6 to 6
- first_gain: bfloat16 [2560], P(('seq', 'fsdp')), may hold values from 0.5 to 1.5
- branch_weight: bfloat16 [2560, 2560], P(('seq', 'fsdp')), may hold values from -0.125 to 0.125
- input_weight: bfloat16 [2560, 2560], P(('seq', 'fsdp')), may hold values from -0.125 to 0.125
- conv_weight: bfloat16 [2560, 4], P(('seq', 'fsdp')), may hold values from -3 to 3
- input_gate: bfloat16 [2560, 256], P(('seq', 'fsdp')), may hold values from -0.375 to 0.375
- decay_gate: bfloat16 [2560, 256], P(('seq', 'fsdp')), may hold values from -0.375 to 0.375
- decay_param: bfloat16 [2560], P(('seq', 'fsdp')), may hold values from -14 to -4
- output_weight: bfloat16 [2560, 2560], P(('seq', 'fsdp')), may hold values from -0.25 to 0.25
- second_gain: bfloat16 [2560], P(('seq', 'fsdp')), may hold values from 0.5 to 1.5
- gate_weight: bfloat16 [2560, 7680], P(('seq', 'fsdp')), may hold values from -0.125 to 0.125
- up_weight: bfloat16 [2560, 7680], P(('seq', 'fsdp')), may hold values from -0.125 to 0.125
- down_weight: bfloat16 [2560, 7680], P(('seq', 'fsdp')), may hold values from -0.0625 to 0.0625
Outputs:
- result: bfloat16 [4, 1024, 2560], P('fsdp', 'seq')
- grad_inputs: bfloat16 [4, 1024, 2560], P('fsdp', 'seq')
- grad_first_gain: float32 [2560], P(('seq', 'fsdp'))
- grad_branch_weight: float32 [2560, 2560], P(('seq', 'fsdp'))
- grad_input_weight: float32 [2560, 2560], P(('seq', 'fsdp'))
- grad_conv_weight: float32 [2560, 4], P(('seq', 'fsdp'))
- grad_input_gate: float32 [2560, 256], P(('seq', 'fsdp'))
- grad_decay_gate: float32 [2560, 256], P(('seq', 'fsdp'))
- grad_decay_param: float32 [2560], P(('seq', 'fsdp'))
- grad_output_weight: float32 [2560, 2560], P(('seq', 'fsdp'))
- grad_second_gain: float32 [2560], P(('seq', 'fsdp'))
- grad_gate_weight: float32 [2560, 7680], P(('seq', 'fsdp'))
- grad_up_weight: float32 [2560, 7680], P(('seq', 'fsdp'))
- grad_down_weight: float32 [2560, 7680], P(('seq', 'fsdp'))
Inputs may be any that keep to these rules, and one draw needn't show every extreme that they name: `resets`: each group's first token is 1. In each group one document starts within its first 64 tokens and ends within its last 64, with no other 1 in between.
All inputs are finite; a program needn't handle non-finite values.
Results may differ from a plain program's by a relative error of at most 0.012.
Values may be sent and summed in bfloat16 or wider, within the bound.
A program may use at most 1 GiB of HBM per device.

v0:
```python
import jax
import jax.numpy as jnp
from jax import lax
from jax.experimental import pallas as pl
from jax.experimental.pallas import tpu as pltpu
from jax.sharding import PartitionSpec as P

EPSILON = 1e-06
CONTRACT_ROWS = (((0,), (0,)), ((), ()))
CONTRACT_LAST = (((1,), (1,)), ((), ()))


def shifted_2(value, axis, steps):
    count = lax.axis_size(axis)
    leading, last = (max(0, -steps), min(count, count - steps))
    return lax.ppermute(value, axis, [(source, source + steps) for source in range(leading, last)])


def entering(x, axis, combine, identity, reverse):
    peers, index = (lax.axis_size(axis), lax.axis_index(axis))
    everything = jax.tree.map(lambda part: lax.all_gather(part, axis), x)
    start = jax.tree.map(
        lambda part, zero: jnp.broadcast_to(jnp.asarray(zero, part.dtype), part.shape), x, identity
    )

    def lap(k, before):
        at = peers - 1 - k if reverse else k
        reached = at > index if reverse else at < index
        new = combine(before, jax.tree.map(lambda part: part[at], everything))
        return jax.tree.map(lambda a, b: jnp.where(reached, a, b), new, before)

    return lax.fori_loop(0, peers, lap, start)


def affine(earlier, later):
    return (earlier[0] * later[0], later[0] * earlier[1] + later[1])


def product(operand_one, operand_two):
    return jnp.dot(operand_one, operand_two, preferred_element_type=jnp.float32)


def rows_product(operand_one, operand_two):
    return lax.dot_general(
        operand_one, operand_two, CONTRACT_ROWS, preferred_element_type=jnp.float32
    )


def last_product(operand_one, operand_two):
    return lax.dot_general(
        operand_one, operand_two, CONTRACT_LAST, preferred_element_type=jnp.float32
    )


def heads_apply(values, weight, head_count):
    token_count = values.shape[0]
    head_width = weight.shape[1]
    shaped = values.reshape(token_count, head_count, head_width)
    blocks = weight.reshape(head_count, head_width, head_width)
    mixed = jnp.einsum("thi,hij->thj", shaped, blocks, preferred_element_type=jnp.float32)
    return mixed.reshape(token_count, head_count * head_width)


def heads_back(gradients, weight, head_count):
    token_count = gradients.shape[0]
    head_width = weight.shape[1]
    shaped = gradients.reshape(token_count, head_count, head_width)
    blocks = weight.reshape(head_count, head_width, head_width)
    mixed = jnp.einsum("thj,hij->thi", shaped, blocks, preferred_element_type=jnp.float32)
    return mixed.reshape(token_count, head_count * head_width)


def heads_grad(values, gradients, head_count):
    token_count = values.shape[0]
    head_width = values.shape[1] // head_count
    left_side = values.reshape(token_count, head_count, head_width)
    right_side = gradients.reshape(token_count, head_count, head_width)
    summed = jnp.einsum("thi,thj->hij", left_side, right_side, preferred_element_type=jnp.float32)
    return summed.reshape(head_count * head_width, head_width)


def slab_count():
    for candidate in (5, 4, 2):
        return candidate
    return 1


def local(
    inputs,
    resets,
    cotangent,
    first_gain,
    branch_weight,
    input_weight,
    conv_weight,
    input_gate,
    decay_gate,
    decay_param,
    output_weight,
    second_gain,
    gate_weight,
    up_weight,
    down_weight,
):
    sources = inputs[0].astype(jnp.float32)
    flags = resets[0]
    returned = cotangent[0]
    returned_float = returned.astype(jnp.float32)
    tokens = sources.shape[0]
    shared = (
        lax.all_gather(first_gain, ("seq", "fsdp"), axis=0, tiled=True),
        lax.all_gather(branch_weight, ("seq", "fsdp"), axis=0, tiled=True),
        lax.all_gather(input_weight, ("seq", "fsdp"), axis=0, tiled=True),
        lax.all_gather(conv_weight, ("seq", "fsdp"), axis=0, tiled=True),
        lax.all_gather(input_gate, ("seq", "fsdp"), axis=0, tiled=True),
        lax.all_gather(decay_gate, ("seq", "fsdp"), axis=0, tiled=True),
        lax.all_gather(decay_param, ("seq", "fsdp"), axis=0, tiled=True),
        lax.all_gather(output_weight, ("seq", "fsdp"), axis=0, tiled=True),
        lax.all_gather(second_gain, ("seq", "fsdp"), axis=0, tiled=True),
    )
    dense_parts = (
        lax.all_gather(gate_weight, ("seq", "fsdp"), axis=0, tiled=True),
        lax.all_gather(up_weight, ("seq", "fsdp"), axis=0, tiled=True),
        lax.all_gather(down_weight, ("seq", "fsdp"), axis=0, tiled=True),
    )
    gain_first = shared[0].astype(jnp.float32)
    w_branch = shared[1]
    w_input = shared[2]
    w_conv = shared[3].astype(jnp.float32)
    w_igate = shared[4]
    w_dgate = shared[5]
    w_decay = shared[6].astype(jnp.float32)
    w_output = shared[7]
    gain_second = shared[8].astype(jnp.float32)
    w_gate = dense_parts[0]
    w_up = dense_parts[1]
    w_down = dense_parts[2]
    model_width = w_branch.shape[0]
    head_width = w_igate.shape[1]
    head_count = model_width // head_width
    tap_count = w_conv.shape[1]
    scale_one = lax.rsqrt(jnp.mean(sources * sources, axis=1, keepdims=True) + EPSILON)
    normed = (sources * scale_one * gain_first).astype(jnp.bfloat16)
    branch_pre = product(normed, w_branch)
    branch, branch_pull = jax.vjp(jax.nn.gelu, branch_pre)
    conv_in = product(normed, w_input).astype(jnp.bfloat16)
    resets_seen = jnp.cumsum(flags)
    tail_keep = resets_seen[-1] - resets_seen[tokens - tap_count + 1 :] == 0
    tail_rows = conv_in[tokens - tap_count + 1 :] * tail_keep[:, None]
    before = shifted_2(tail_rows, "seq", 1)
    padded = jnp.concatenate([before, conv_in], axis=0)
    seen_before = jnp.concatenate([jnp.zeros((tap_count - 1,), jnp.int32), resets_seen])
    conv_out = jnp.zeros((tokens, model_width), jnp.float32)
    usable_list = []
    for offset in range(tap_count):
        first_row = tap_count - 1 - offset
        shifted = padded[first_row : first_row + tokens].astype(jnp.float32)
        usable = (resets_seen - seen_before[first_row : first_row + tokens] == 0).astype(
            jnp.float32
        )[:, None]
        usable_list.append(usable)
        conv_out = conv_out + w_conv[:, offset] * shifted * usable
    rounded = conv_out.astype(jnp.bfloat16)
    rounded_float = rounded.astype(jnp.float32)
    gate_input = jax.nn.sigmoid(heads_apply(rounded, w_igate, head_count))
    gate_decay = jax.nn.sigmoid(heads_apply(rounded, w_dgate, head_count))
    softened = jax.nn.softplus(w_decay)
    log_decay = -softened * (1.0 + 7.0 * gate_decay)
    decays = jnp.exp(log_decay)
    root_term = jnp.sqrt(-jnp.expm1(2.0 * log_decay))
    restart = flags.astype(jnp.float32)[:, None]
    carried = 1.0 - restart
    scaling = restart + carried * root_term
    driven = rounded_float * gate_input * scaling
    coefficient = decays * carried
    running, local_state = lax.associative_scan(affine, (coefficient, driven), axis=0)
    unit_ones = jnp.ones((model_width,), jnp.float32)
    unit_zeros = jnp.zeros((model_width,), jnp.float32)
    incoming = entering(
        (running[-1], local_state[-1]), "seq", affine, (unit_ones, unit_zeros), False
    )
    state_in = incoming[1]
    states = local_state + running * state_in
    mixed = (states * branch).astype(jnp.bfloat16)
    resid = sources + product(mixed, w_output)
    scale_two = lax.rsqrt(jnp.mean(resid * resid, axis=1, keepdims=True) + EPSILON)
    hidden = (resid * scale_two * gain_second).astype(jnp.bfloat16)
    gate_pre = product(hidden, w_gate)
    up_values = product(hidden, w_up)
    gate_act, gate_pull = jax.vjp(jax.nn.gelu, gate_pre)
    active = (gate_act * up_values).astype(jnp.bfloat16)
    result = (resid + last_product(active, w_down)).astype(jnp.bfloat16)
    act_grad = product(returned, w_down)
    gate_grad = gate_pull(act_grad * up_values)[0].astype(jnp.bfloat16)
    up_grad = (act_grad * gate_act).astype(jnp.bfloat16)
    hidden_grad = last_product(gate_grad, w_gate) + last_product(up_grad, w_up)
    weighted_two = hidden_grad * gain_second
    resid_grad = (
        returned_float
        + scale_two * weighted_two
        - resid * scale_two**3 * jnp.mean(weighted_two * resid, axis=1, keepdims=True)
    )
    second_term = jnp.sum(hidden_grad * resid * scale_two, axis=0)
    branch_out_grad = resid_grad.astype(jnp.bfloat16)
    mixed_grad = last_product(branch_out_grad, w_output)
    state_grad = mixed_grad * branch
    branch_grad = mixed_grad * states
    branch_pre_grad = branch_pull(branch_grad)[0].astype(jnp.bfloat16)
    next_coef = jnp.concatenate([coefficient[1:], jnp.ones((1, model_width), jnp.float32)], axis=0)
    reaches, adjoint_local = lax.associative_scan(
        affine, (next_coef, state_grad), reverse=True, axis=0
    )
    carry_back = entering(
        (coefficient[0] * reaches[0], coefficient[0] * adjoint_local[0]),
        "seq",
        affine,
        (unit_ones, unit_zeros),
        True,
    )
    adjoint = adjoint_local + reaches * carry_back[1]
    earlier_state = jnp.concatenate([state_in[None], states[:-1]], axis=0)
    log_grad = (
        adjoint * earlier_state * carried * decays
        - adjoint * rounded_float * gate_input * carried * decays * decays / root_term
    )
    decay_term = jnp.sum(-log_grad * (1.0 + 7.0 * gate_decay), axis=0) * jax.nn.sigmoid(w_decay)
    input_pre_grad = (adjoint * rounded_float * scaling * gate_input * (1.0 - gate_input)).astype(
        jnp.bfloat16
    )
    decay_pre_grad = (log_grad * (-7.0 * softened) * gate_decay * (1.0 - gate_decay)).astype(
        jnp.bfloat16
    )
    conv_out_grad = (
        adjoint * gate_input * scaling
        + heads_back(input_pre_grad, w_igate, head_count)
        + heads_back(decay_pre_grad, w_dgate, head_count)
    )
    conv_grad = conv_out_grad.astype(jnp.bfloat16)
    igate_term = heads_grad(rounded, input_pre_grad, head_count)
    dgate_term = heads_grad(rounded, decay_pre_grad, head_count)
    head_keep = resets_seen[: tap_count - 1] == 0
    head_rows = conv_grad[: tap_count - 1] * head_keep[:, None]
    following = shifted_2(head_rows, "seq", -1)
    padded_back = jnp.concatenate([conv_grad, following], axis=0)
    seen_after = jnp.concatenate(
        [resets_seen, jnp.full((tap_count - 1,), resets_seen[-1], jnp.int32)]
    )
    conv_grad_float = conv_grad.astype(jnp.float32)
    conv_in_grad = jnp.zeros((tokens, model_width), jnp.float32)
    tap_terms = []
    for offset in range(tap_count):
        first_row = tap_count - 1 - offset
        shifted = padded[first_row : first_row + tokens].astype(jnp.float32)
        tap_terms.append(jnp.sum(conv_grad_float * shifted * usable_list[offset], axis=0))
        ahead_usable = (seen_after[offset : offset + tokens] - resets_seen == 0).astype(
            jnp.float32
        )[:, None]
        conv_in_grad = (
            conv_in_grad
            + w_conv[:, offset]
            * padded_back[offset : offset + tokens].astype(jnp.float32)
            * ahead_usable
        )
    tap_grad = jnp.stack(tap_terms, axis=1)
    conv_in_low = conv_in_grad.astype(jnp.bfloat16)
    normed_grad = last_product(branch_pre_grad, w_branch) + last_product(conv_in_low, w_input)
    weighted_one = normed_grad * gain_first
    source_grad = (
        resid_grad
        + scale_one * weighted_one
        - sources * scale_one**3 * jnp.mean(weighted_one * sources, axis=1, keepdims=True)
    )
    first_term = jnp.sum(normed_grad * sources * scale_one, axis=0)
    grad_inputs = source_grad.astype(jnp.bfloat16)[None]
    vector_part = jnp.concatenate(
        [
            igate_term,
            dgate_term,
            tap_grad,
            decay_term[:, None],
            first_term[:, None],
            second_term[:, None],
        ],
        axis=1,
    )
    owned_rows = gate_weight.shape[0]
    owner_count = lax.axis_size(("seq", "fsdp"))
    slab_total = slab_count()
    slab_rows = owned_rows // slab_total
    vector_shaped = vector_part.reshape(owner_count, owned_rows, vector_part.shape[1])

    def pick_rows(values, portion):
        shaped = values.reshape(values.shape[0], owner_count, owned_rows)
        taken = shaped[:, :, portion * slab_rows : (portion + 1) * slab_rows]
        return taken.reshape(values.shape[0], owner_count * slab_rows)

    gate_pieces = []
    up_pieces = []
    down_pieces = []
    branch_pieces = []
    input_pieces = []
    output_pieces = []
    vector_pieces = []
    for portion in range(slab_total):
        hidden_rows = pick_rows(hidden, portion)
        return_rows = pick_rows(returned, portion)
        dense_sums = (
            lax.psum_scatter(
                rows_product(hidden_rows, gate_grad),
                ("seq", "fsdp"),
                scatter_dimension=0,
                tiled=True,
            ),
            lax.psum_scatter(
                rows_product(hidden_rows, up_grad), ("seq", "fsdp"), scatter_dimension=0, tiled=True
            ),
            lax.psum_scatter(
                rows_product(return_rows, active), ("seq", "fsdp"), scatter_dimension=0, tiled=True
            ),
        )
        gate_pieces.append(dense_sums[0])
        up_pieces.append(dense_sums[1])
        down_pieces.append(dense_sums[2])
        normed_rows = pick_rows(normed, portion)
        mixed_rows = pick_rows(mixed, portion)
        vector_rows = vector_shaped[:, portion * slab_rows : (portion + 1) * slab_rows].reshape(
            owner_count * slab_rows, vector_part.shape[1]
        )
        mixer_sums = (
            lax.psum_scatter(
                rows_product(normed_rows, branch_pre_grad),
                ("seq", "fsdp"),
                scatter_dimension=0,
                tiled=True,
            ),
            lax.psum_scatter(
                rows_product(normed_rows, conv_in_low),
                ("seq", "fsdp"),
                scatter_dimension=0,
                tiled=True,
            ),
            lax.psum_scatter(
                rows_product(mixed_rows, branch_out_grad),
                ("seq", "fsdp"),
                scatter_dimension=0,
                tiled=True,
            ),
            lax.psum_scatter(vector_rows, ("seq", "fsdp"), scatter_dimension=0, tiled=True),
        )
        branch_pieces.append(mixer_sums[0])
        input_pieces.append(mixer_sums[1])
        output_pieces.append(mixer_sums[2])
        vector_pieces.append(mixer_sums[3])
    grad_gate = jnp.concatenate(gate_pieces, axis=0)
    grad_up = jnp.concatenate(up_pieces, axis=0)
    grad_down = jnp.concatenate(down_pieces, axis=0)
    grad_branch = jnp.concatenate(branch_pieces, axis=0)
    grad_input = jnp.concatenate(input_pieces, axis=0)
    grad_output = jnp.concatenate(output_pieces, axis=0)
    vector_sums = jnp.concatenate(vector_pieces, axis=0)
    edge_five = 2 * head_width
    edge_six = edge_five + tap_count
    grad_igate = vector_sums[:, :head_width]
    grad_dgate = vector_sums[:, head_width:edge_five]
    grad_conv = vector_sums[:, edge_five:edge_six]
    grad_decay = vector_sums[:, edge_six]
    grad_gain_first = vector_sums[:, edge_six + 1]
    grad_gain_second = vector_sums[:, edge_six + 2]
    return (
        result[None],
        grad_inputs,
        grad_gain_first,
        grad_branch,
        grad_input,
        grad_conv,
        grad_igate,
        grad_dgate,
        grad_decay,
        grad_output,
        grad_gain_second,
        grad_gate,
        grad_up,
        grad_down,
    )


CHUNK = 128
TAPS = 4


def gelu_parts(x):
    inner = 0.7978845608028654 * (x + 0.044715 * x * x * x)
    bent = jnp.tanh(inner)
    value = 0.5 * x * (1.0 + bent)
    slope = 0.5 * (1.0 + bent) + 0.5 * x * (1.0 - bent * bent) * 0.7978845608028654 * (
        1.0 + 3.0 * 0.044715 * x * x
    )
    return value, slope


def minus_expm1(x):
    series = x / 8.0 + 1.0
    for step in (7.0, 6.0, 5.0, 4.0, 3.0, 2.0):
        series = series * x / step + 1.0
    return jnp.where(x > -0.5, -x * series, 1.0 - jnp.exp(x))


def mixer_forward_kernel(
    conv_in_ref, pre_ref, mask_ref, taps_ref, igate_ref, dgate_ref, soft_ref,
    rounded_ref, gin_ref, gdec_ref, states_ref, earlier_ref, mixed_ref,
    padded, coef, drive,
):
    tokens, width = conv_in_ref.shape
    chunk = min(CHUNK, tokens)
    padded[0:8, :] = jnp.zeros((8, width), jnp.float32)
    soft = soft_ref[0:1, :]
    igate = igate_ref[...]
    dgate = dgate_ref[...]

    def fill(c, _):
        base = pl.multiple_of(c * chunk, chunk)
        padded[pl.ds(pl.multiple_of(base + 8, 8), chunk), :] = conv_in_ref[pl.ds(base, chunk), :].astype(jnp.float32)
        return 0

    lax.fori_loop(0, tokens // chunk, fill, 0)
    row = lax.broadcasted_iota(jnp.int32, (8, width), 0)

    def body(c, carry):
        base = pl.multiple_of(c * chunk, chunk)
        mask = mask_ref[pl.ds(base, chunk), :]
        span = padded[pl.ds(base, chunk + 8), :]
        out = taps_ref[0:1, :] * span[8:]
        for k in range(1, TAPS):
            out = out + taps_ref[k : k + 1, :] * span[8 - k : 8 - k + chunk] * mask[:, k : k + 1]
        rounded = out.astype(jnp.bfloat16)
        rounded_ref[pl.ds(base, chunk), :] = rounded
        gin = jax.nn.sigmoid(jnp.dot(rounded, igate, preferred_element_type=jnp.float32))
        gdec = jax.nn.sigmoid(jnp.dot(rounded, dgate, preferred_element_type=jnp.float32))
        gin_ref[pl.ds(base, chunk), :] = gin
        gdec_ref[pl.ds(base, chunk), :] = gdec
        log_decay = -soft * (1.0 + 7.0 * gdec)
        root = jnp.sqrt(minus_expm1(2.0 * log_decay))
        restart = mask[:, 0:1]
        carried = 1.0 - restart
        coef[...] = jnp.exp(log_decay) * carried
        drive[...] = rounded.astype(jnp.float32) * gin * (restart + carried * root)

        def tile(i, state):
            at = pl.multiple_of(i * 8, 8)
            a = coef[pl.ds(at, 8), :]
            b = drive[pl.ds(at, 8), :]
            for sh in (1, 2, 4):
                keep = row >= sh
                b = b + a * jnp.where(keep, pltpu.roll(b, sh, 0), 0.0)
                a = a * jnp.where(keep, pltpu.roll(a, sh, 0), 1.0)
            new = b + a * state
            states_ref[pl.ds(pl.multiple_of(base + at, 8), 8), :] = new
            earlier_ref[pl.ds(pl.multiple_of(base + at, 8), 8), :] = jnp.where(row == 0, state, pltpu.roll(new, 1, 0))
            return jnp.broadcast_to(new[7:8, :], (8, width))

        carry = lax.fori_loop(0, chunk // 8, tile, carry, unroll=True)
        branch, _ = gelu_parts(pre_ref[pl.ds(base, chunk), :])
        mixed_ref[pl.ds(base, chunk), :] = (states_ref[pl.ds(base, chunk), :] * branch).astype(jnp.bfloat16)
        return carry

    lax.fori_loop(0, tokens // chunk, body, jnp.zeros((8, width), jnp.float32))


def mixer_forward(conv_in, pre, mask, taps, igate, dgate, soft, width):
    tokens, total = conv_in.shape
    heads = total // width
    column = lambda h: (0, h)
    row = lambda h: (h, 0)
    whole = lambda h: (0, 0)
    big = pl.BlockSpec((tokens, width), column)
    shape = lambda kind: jax.ShapeDtypeStruct((tokens, total), kind)
    return pl.pallas_call(
        mixer_forward_kernel,
        grid=(heads,),
        in_specs=[
            big, big, pl.BlockSpec(mask.shape, whole), pl.BlockSpec((8, width), column),
            pl.BlockSpec((width, width), row), pl.BlockSpec((width, width), row),
            pl.BlockSpec((8, width), column),
        ],
        out_specs=[big] * 6,
        out_shape=[shape(jnp.bfloat16), shape(jnp.float32), shape(jnp.float32), shape(jnp.float32), shape(jnp.float32), shape(jnp.bfloat16)],
        scratch_shapes=[
            pltpu.VMEM((tokens + 8, width), jnp.float32),
            pltpu.VMEM((min(CHUNK, tokens), width), jnp.float32),
            pltpu.VMEM((min(CHUNK, tokens), width), jnp.float32),
        ],
        compiler_params=pltpu.CompilerParams(vmem_limit_bytes=48 * 2**20),
        name="mixer_forward",
    )(conv_in, pre, mask, taps, igate, dgate, soft)


def mixer_backward_kernel(
    grad_ref, pre_ref, states_ref, earlier_ref, rounded_ref, gin_ref, gdec_ref, conv_in_ref, mask_ref, ahead_ref,
    taps_ref, igate_ref, dgate_ref, soft_ref, own_ref,
    bpg_ref, cig_ref, igrad_ref, dgrad_ref, tapgrad_ref,
    padded, ahead_pad, coef, drive, decay_sum, tap_sum,
):
    tokens, width = grad_ref.shape
    chunk = min(CHUNK, tokens)
    count = tokens // chunk
    padded[0:8, :] = jnp.zeros((8, width), jnp.float32)
    ahead_pad[tokens : tokens + 8, :] = jnp.zeros((8, width), jnp.float32)
    soft = soft_ref[0:1, :]
    own = own_ref[0:1, :]
    igate = igate_ref[...]
    dgate = dgate_ref[...]
    igrad_ref[...] = jnp.zeros_like(igrad_ref)
    dgrad_ref[...] = jnp.zeros_like(dgrad_ref)
    decay_sum[...] = jnp.zeros_like(decay_sum)
    tap_sum[...] = jnp.zeros_like(tap_sum)
    row = lax.broadcasted_iota(jnp.int32, (8, width), 0)
    rows_dot = lambda a, b: lax.dot_general(a, b, (((0,), (0,)), ((), ())), preferred_element_type=jnp.float32)
    last_dot = lambda a, b: lax.dot_general(a, b, (((1,), (1,)), ((), ())), preferred_element_type=jnp.float32)

    def body(step, carry):
        c = count - 1 - step
        base = pl.multiple_of(c * chunk, chunk)
        here = pl.ds(base, chunk)
        padded[pl.ds(pl.multiple_of(base + 8, 8), chunk), :] = conv_in_ref[here, :].astype(jnp.float32)
        mask = mask_ref[here, :]
        restart = mask[:, 0:1]
        carried = 1.0 - restart
        branch, slope = gelu_parts(pre_ref[here, :])
        grad = grad_ref[here, :]
        bpg_ref[here, :] = (grad * states_ref[here, :] * slope * own).astype(jnp.bfloat16)
        gdec = gdec_ref[here, :]
        gin = gin_ref[here, :]
        log_decay = -soft * (1.0 + 7.0 * gdec)
        decays = jnp.exp(log_decay)
        root = jnp.sqrt(minus_expm1(2.0 * log_decay))
        coef[...] = decays * carried
        drive[...] = grad * branch

        def tile(i, pair):
            adj_next, coef_next = pair
            at = pl.multiple_of(chunk - 8 - i * 8, 8)
            first = coef[pl.ds(at, 8), :]
            a = jnp.where(row == 7, coef_next, pltpu.roll(first, 7, 0))
            b = drive[pl.ds(at, 8), :]
            for sh in (1, 2, 4):
                keep = row < 8 - sh
                b = b + a * jnp.where(keep, pltpu.roll(b, 8 - sh, 0), 0.0)
                a = a * jnp.where(keep, pltpu.roll(a, 8 - sh, 0), 1.0)
            new = b + a * adj_next
            drive[pl.ds(at, 8), :] = new
            return jnp.broadcast_to(new[0:1, :], (8, width)), jnp.broadcast_to(first[0:1, :], (8, width))

        carry = lax.fori_loop(0, chunk // 8, tile, carry, unroll=True)
        adjoint = drive[...]
        rounded = rounded_ref[here, :]
        rounded_float = rounded.astype(jnp.float32)
        pull = adjoint * carried * decays
        log_grad = pull * (earlier_ref[here, :] - rounded_float * gin * decays / root)
        decay_sum[...] += jnp.sum((-log_grad * (1.0 + 7.0 * gdec)).reshape(chunk // 8, 8, width), axis=0)
        through = adjoint * gin * (restart + carried * root)
        ipg = (through * rounded_float * (1.0 - gin)).astype(jnp.bfloat16)
        dpg = (log_grad * (-7.0 * soft) * gdec * (1.0 - gdec)).astype(jnp.bfloat16)
        igrad_ref[...] += rows_dot(rounded, ipg)
        dgrad_ref[...] += rows_dot(rounded, dpg)
        through = through + last_dot(ipg, igate) + last_dot(dpg, dgate)
        ahead_pad[here, :] = through.astype(jnp.bfloat16).astype(jnp.float32)
        return carry

    zero = jnp.zeros((8, width), jnp.float32)
    lax.fori_loop(0, count, body, (zero, zero))

    def after(c, _):
        base = pl.multiple_of(c * chunk, chunk)
        here = pl.ds(base, chunk)
        mask = mask_ref[here, :]
        ahead = ahead_ref[here, :]
        later = ahead_pad[pl.ds(base, chunk + 8), :]
        span = padded[pl.ds(base, chunk + 8), :]
        grad = later[:chunk]
        total = taps_ref[0:1, :] * grad
        tap_sum[0:8, :] += jnp.sum((grad * span[8:]).reshape(chunk // 8, 8, width), axis=0)
        for k in range(1, TAPS):
            total = total + taps_ref[k : k + 1, :] * later[k : k + chunk] * ahead[:, k : k + 1]
            shifted = span[8 - k : 8 - k + chunk]
            tap_sum[8 * k : 8 * k + 8, :] += jnp.sum((grad * shifted * mask[:, k : k + 1]).reshape(chunk // 8, 8, width), axis=0)
        cig_ref[here, :] = (total * own).astype(jnp.bfloat16)
        return 0

    lax.fori_loop(0, count, after, 0)
    for k in range(TAPS):
        tapgrad_ref[k : k + 1, :] = jnp.sum(tap_sum[8 * k : 8 * k + 8, :], axis=0, keepdims=True)
    tapgrad_ref[4:5, :] = jnp.sum(decay_sum[...], axis=0, keepdims=True)
    tapgrad_ref[5:8, :] = jnp.zeros((3, width), jnp.float32)


def mixer_backward(grad, pre, states, earlier, rounded, gin, gdec, conv_in, mask, ahead, taps, igate, dgate, soft, own, width):
    tokens, total = grad.shape
    heads = total // width
    column = lambda h: (0, h)
    row = lambda h: (h, 0)
    whole = lambda h: (0, 0)
    big = pl.BlockSpec((tokens, width), column)
    line = pl.BlockSpec((8, width), column)
    square = pl.BlockSpec((width, width), row)
    shape = lambda kind: jax.ShapeDtypeStruct((tokens, total), kind)
    chunk = min(CHUNK, tokens)
    return pl.pallas_call(
        mixer_backward_kernel,
        grid=(heads,),
        in_specs=[big] * 8 + [pl.BlockSpec(mask.shape, whole)] * 2 + [line, square, square, line, line],
        out_specs=[big, big, square, square, line],
        out_shape=[
            shape(jnp.bfloat16), shape(jnp.bfloat16),
            jax.ShapeDtypeStruct((total, width), jnp.float32), jax.ShapeDtypeStruct((total, width), jnp.float32),
            jax.ShapeDtypeStruct((8, total), jnp.float32),
        ],
        scratch_shapes=[
            pltpu.VMEM((tokens + 8, width), jnp.float32),
            pltpu.VMEM((tokens + 8, width), jnp.float32),
            pltpu.VMEM((chunk, width), jnp.float32),
            pltpu.VMEM((chunk, width), jnp.float32),
            pltpu.VMEM((8, width), jnp.float32),
            pltpu.VMEM((8 * TAPS, width), jnp.float32),
        ],
        compiler_params=pltpu.CompilerParams(vmem_limit_bytes=56 * 2**20),
        name="mixer_backward",
    )(grad, pre, states, earlier, rounded, gin, gdec, conv_in, mask, ahead, taps, igate, dgate, soft, own)


MESH_ID = pl.DeviceIdType.MESH
PIECES = 4


class Spot:
    def __init__(self):
        self.s = lax.axis_index("seq")
        self.f = lax.axis_index("fsdp")
        self.z = self.s // 2
        self.y = self.s % 2
        self.up = (self.z < 3, (jnp.minimum(self.s + 2, 7), self.f))
        self.down = (self.z > 0, (jnp.maximum(self.s - 2, 0), self.f))
        self.beside = (None, (self.s ^ 1, self.f))
        self.across = (None, (self.s, self.f ^ 2))
        self.twin = (None, (self.s, self.f ^ 1))

    def peer(self, j):
        return (None, (self.s ^ j, self.f))

    def other(self, j):
        return (None, (self.s ^ (j // 4), self.f ^ (j % 4)))

    def meet(self, reach):
        barrier = pltpu.get_barrier_semaphore()
        if "all" in reach:
            peers = [self.other(j) for j in range(1, 32)]
        else:
            peers = [self.peer(j) for j in range(1, 8)] if "seq" in reach else []
            if "line" in reach and not peers:
                peers = [self.up, self.down, self.beside]
            if "pair" in reach:
                peers += [self.across, self.twin]
        count = 0
        for cond, where in peers:
            count = count + (1 if cond is None else cond.astype(jnp.int32))
            guarded(cond, lambda: pl.semaphore_signal(barrier, 1, device_id=where, device_id_type=MESH_ID))
        pl.semaphore_wait(barrier, count)


def guarded(cond, action):
    if cond is None:
        action()
    else:
        pl.when(cond)(action)


class Send:
    def __init__(self, src, dst, send_sem, recv_sem, target):
        self.cond, where = target
        self.copy = pltpu.make_async_remote_copy(
            src_ref=src, dst_ref=dst, send_sem=send_sem, recv_sem=recv_sem, device_id=where, device_id_type=MESH_ID
        )

    def start(self):
        guarded(self.cond, self.copy.start)

    def sent(self):
        guarded(self.cond, self.copy.wait_send)


def arrived(dst, send_sem, recv_sem, target, cond=None):
    copy = pltpu.make_async_remote_copy(
        src_ref=dst, dst_ref=dst, send_sem=send_sem, recv_sem=recv_sem, device_id=target[1], device_id_type=MESH_ID
    )
    guarded(cond, copy.wait_recv)


class Gather:
    letter = "g"
    def __init__(self, x):
        self.ins = [x]
        self.outs = [jax.ShapeDtypeStruct((8,) + x.shape, x.dtype)]
        dma = pltpu.SemaphoreType.DMA
        self.scratch = [dma((1,)), dma((8, PIECES)), dma((4, PIECES)), dma((4, PIECES)), dma((7, PIECES))]

    reach = ("line",)

    def steps(self, at, ins, outs, scratch):
        (x,), (o,) = ins, outs
        own_sem, recv, ups, downs, sides = scratch
        rows = x.shape[0] // PIECES
        cut = lambda p: pl.ds(p * rows, rows)
        sends = []

        def send(src, block, p, sem, target):
            one = Send(src, o.at[block, cut(p)], sem, recv.at[block, p], target)
            one.start()
            sends.append(one)

        own = pltpu.make_async_copy(x, o.at[at.s], own_sem.at[0])
        own.start()
        for p in range(PIECES):
            send(x.at[cut(p)], at.s, p, ups.at[0, p], at.up)
            send(x.at[cut(p)], at.s, p, downs.at[0, p], at.down)
            send(x.at[cut(p)], at.s, p, sides.at[0, p], at.beside)
        yield
        for d in range(1, 4):
            for p in range(PIECES):
                low, high = at.z >= d, at.z + d <= 3
                block = jnp.maximum(at.s - 2 * d, 0)
                arrived(o.at[block, cut(p)], ups.at[0, p], recv.at[block, p], at.down, low)
                if d < 3:
                    send(o.at[block, cut(p)], block, p, ups.at[d, p], (low & (at.z < 3), at.up[1]))
                send(o.at[block, cut(p)], block, p, sides.at[d, p], (low, at.beside[1]))
                block = jnp.minimum(at.s + 2 * d, 7)
                arrived(o.at[block, cut(p)], ups.at[0, p], recv.at[block, p], at.up, high)
                if d < 3:
                    send(o.at[block, cut(p)], block, p, downs.at[d, p], (high & (at.z > 0), at.down[1]))
                send(o.at[block, cut(p)], block, p, sides.at[3 + d, p], (high, at.beside[1]))
                yield
        for z in range(4):
            for p in range(PIECES):
                block = 2 * z + 1 - at.y
                arrived(o.at[block, cut(p)], ups.at[0, p], recv.at[block, p], at.beside)
        yield
        for one in sends:
            one.sent()
        own.wait()


class Reduce:
    letter = "r"
    def __init__(self, x):
        _, rows, width = x.shape
        self.ins = [x]
        self.outs = [jax.ShapeDtypeStruct((rows, width), jnp.float32)]
        dma = pltpu.SemaphoreType.DMA
        hold = pltpu.VMEM((4, rows, width), x.dtype)
        self.scratch = [hold, hold, hold, hold, pltpu.VMEM((rows, width), jnp.float32)]
        self.scratch += [dma((4, PIECES)) for _ in range(6)] + [dma((1,))]

    reach = ("line",)

    def steps(self, at, ins, outs, scratch):
        (x,), (o,) = ins, outs
        mine, side, below, above, total, load, ysend, yrecv, zsend, urecv, drecv, osem = scratch
        rows = x.shape[1] // PIECES
        cut = lambda p: pl.ds(p * rows, rows)
        group = 16
        sends = []
        order = []
        for k in range(3):
            order.append((3 - k, at.z < 3 - k, True))
            order.append((k, at.z > k, False))
        order.append((at.z, None, None))

        loads = []
        for t, cond, _ in order:
            for p in range(PIECES):
                one = Send(x.at[2 * t + 1 - at.y, cut(p)], side.at[t, cut(p)], ysend.at[t, p], yrecv.at[t, p], (cond, at.beside[1]))
                one.start()
                sends.append(one)
                copy = pltpu.make_async_copy(x.at[2 * t + at.y, cut(p)], mine.at[t, cut(p)], load.at[t, p])
                guarded(cond, copy.start)
        yield
        for t, cond, rising in order:
            for p in range(PIECES):
                copy = pltpu.make_async_copy(x.at[2 * t + at.y, cut(p)], mine.at[t, cut(p)], load.at[t, p])
                guarded(cond, copy.wait)
                arrived(side.at[t, cut(p)], ysend.at[t, p], yrecv.at[t, p], at.beside, cond)
                if rising is None:
                    arrived(below.at[t, cut(p)], zsend.at[t, p], urecv.at[t, p], at.down, at.z > 0)
                    arrived(above.at[t, cut(p)], zsend.at[t, p], drecv.at[t, p], at.up, at.z < 3)

                    def final(i, _):
                        here = pl.ds(pl.multiple_of(p * rows + i * group, group), group)
                        value = mine[t, here, :].astype(jnp.float32) + side[t, here, :].astype(jnp.float32)
                        total[here, :] = value

                        @pl.when(at.z > 0)
                        def _():
                            total[here, :] += below[t, here, :].astype(jnp.float32)

                        @pl.when(at.z < 3)
                        def _():
                            total[here, :] += above[t, here, :].astype(jnp.float32)

                        return 0

                    lax.fori_loop(0, rows // group, final, 0)
                else:
                    source = below if rising else above
                    inner = (cond & (at.z > 0)) if rising else (cond & (at.z < 3))
                    outer = (cond & (at.z == 0)) if rising else (cond & (at.z == 3))
                    rsem = urecv if rising else drecv
                    arrived(source.at[t, cut(p)], zsend.at[t, p], rsem.at[t, p], at.down if rising else at.up, inner)

                    def add(with_source):
                        def one(i, _):
                            here = pl.ds(pl.multiple_of(p * rows + i * group, group), group)
                            value = mine[t, here, :].astype(jnp.float32) + side[t, here, :].astype(jnp.float32)
                            if with_source:
                                value = value + source[t, here, :].astype(jnp.float32)
                            mine[t, here, :] = value.astype(mine.dtype)
                            return 0

                        lax.fori_loop(0, rows // group, one, 0)

                    pl.when(inner)(lambda: add(True))
                    pl.when(outer)(lambda: add(False))
                    one = Send(mine.at[t, cut(p)], source.at[t, cut(p)], zsend.at[t, p], rsem.at[t, p], (cond, (at.up if rising else at.down)[1]))
                    one.start()
                    sends.append(one)
                yield
        out = pltpu.make_async_copy(total, o, osem.at[0])
        out.start()
        for one in sends:
            one.sent()
        out.wait()


class Spread:
    letter = "s"
    reach = ("seq", "pair")

    def __init__(self, x, starts, wide):
        self.ins = [x]
        self.starts, self.wide = starts, wide
        self.outs = [jax.ShapeDtypeStruct((8, 4, x.shape[0], wide), x.dtype)]
        dma = pltpu.SemaphoreType.DMA
        self.scratch = [dma((8,)), dma((8,)), dma((8,)), dma((8,)), dma((8, 2)), dma((8, 2))]

    def steps(self, at, ins, outs, scratch):
        (x,), (o,) = ins, outs
        asend, arecv, xsend, xrecv, csend, crecv = scratch
        sends = []
        part = lambda to: x.at[:, pl.ds(pl.multiple_of(self.starts(to), 128), self.wide)]

        def send(src, dst, ss, rs, target):
            one = Send(src, dst, ss, rs, target)
            one.start()
            sends.append(one)

        for j in range(1, 8):
            send(part(at.s ^ j), o.at[at.s, at.f], asend.at[j], arecv.at[j], at.peer(j))
        own = pltpu.make_async_copy(part(at.s), o.at[at.s, at.f], asend.at[0])
        own.start()
        yield
        for j in range(8):
            block = at.s ^ j
            here = o.at[block, at.f]
            if j == 0:
                own.wait()
            else:
                arrived(here, asend.at[j], arecv.at[j], at.peer(j))
            send(here, here, xsend.at[j], xrecv.at[j], at.across)
            send(here, here, csend.at[j, 0], crecv.at[j, 0], at.twin)
            yield
        for j in range(8):
            there = o.at[at.s ^ j, at.f ^ 2]
            arrived(there, xsend.at[j], xrecv.at[j], at.across)
            send(there, there, csend.at[j, 1], crecv.at[j, 1], at.twin)
            yield
        for j in range(8):
            for k in range(2):
                arrived(o.at[at.s ^ j, (at.f ^ 1) ^ (2 * k)], csend.at[j, k], crecv.at[j, k], at.twin)
        for one in sends:
            one.sent()


def add_rows(dst, terms, rows):
    group = 16

    def one(i, _):
        here = pl.ds(pl.multiple_of(i * group, group), group)
        value = terms[0][here, :].astype(jnp.float32)
        for term in terms[1:]:
            value = value + term[here, :].astype(jnp.float32)
        dst[here, :] = value.astype(dst.dtype)
        return 0

    lax.fori_loop(0, rows // group, one, 0)


class Collect:
    letter = "c"
    def __init__(self, x):
        blocks, _, rows, width = x.shape
        self.ins = [x]
        self.blocks = blocks
        self.reach = ("seq", "pair") if blocks > 1 else ("pair",)
        self.outs = [jax.ShapeDtypeStruct((blocks, rows, width), x.dtype)]
        dma = pltpu.SemaphoreType.DMA
        hold = pltpu.VMEM((blocks, rows, width), x.dtype)
        self.scratch = [pltpu.VMEM((2, rows, width), x.dtype)] + [hold] * 3 + [dma((2,))] + [dma((blocks, 2))] * 2 + [dma((blocks,))] * 4

    def steps(self, at, ins, outs, scratch):
        (x,), (o,) = ins, outs
        stage, tnear, tfar, xin, lsem, csend, crecv, xsend, xrecv, asend, arecv = scratch
        rows = x.shape[2]
        many = self.blocks > 1
        spot = (lambda j: at.s ^ j) if many else (lambda j: j)
        sends = []

        def send(src, dst, ss, rs, target):
            one = Send(src, dst, ss, rs, target)
            one.start()
            sends.append(one)

        order = [j for j in range(1, 8)] + [0] if many else [0]
        pieces = [(j, at.f ^ 2) for j in order] + [(j, at.f) for j in order]

        def load(i):
            j, whose = pieces[i]
            return pltpu.make_async_copy(x.at[spot(j), whose], stage.at[i % 2], lsem.at[i % 2])

        for j in order:
            send(x.at[spot(j), at.f ^ 3], tfar.at[j], csend.at[j, 0], crecv.at[j, 0], at.twin)
            send(x.at[spot(j), at.f ^ 1], tnear.at[j], csend.at[j, 1], crecv.at[j, 1], at.twin)
        load(0).start()
        yield
        outs_done = []
        for i, (j, _) in enumerate(pieces):
            far = i < len(order)
            if i + 1 < len(pieces):
                load(i + 1).start()
            load(i).wait()
            if far:
                arrived(tfar.at[j], csend.at[j, 0], crecv.at[j, 0], at.twin)
                add_rows(tfar.at[j], (tfar.at[j], stage.at[i % 2]), rows)
                send(tfar.at[j], xin.at[j], xsend.at[j], xrecv.at[j], at.across)
            else:
                arrived(tnear.at[j], csend.at[j, 1], crecv.at[j, 1], at.twin)
                arrived(xin.at[j], xsend.at[j], xrecv.at[j], at.across)
                add_rows(tnear.at[j], (tnear.at[j], stage.at[i % 2], xin.at[j]), rows)
                if j:
                    send(tnear.at[j], o.at[at.s], asend.at[j], arecv.at[j], at.peer(j))
                else:
                    outs_done.append(pltpu.make_async_copy(tnear.at[0], o.at[at.s if many else 0], asend.at[0]))
                    outs_done[-1].start()
            yield
        for j in order:
            if j:
                arrived(o.at[at.s ^ j], asend.at[j], arecv.at[j], at.peer(j))
        for one in sends:
            one.sent()
        for one in outs_done:
            one.wait()


class Tiny:
    letter = "t"
    def __init__(self, x):
        self.ins = [x]
        self.outs = [jax.ShapeDtypeStruct(x.shape, x.dtype)]
        dma = pltpu.SemaphoreType.DMA
        self.scratch = [dma((32,)), dma((32,))]

    reach = ("all",)

    def steps(self, at, ins, outs, scratch):
        (x,), (o,) = ins, outs
        ss, rs = scratch
        me = at.s * 4 + at.f
        sends = []
        for j in range(1, 32):
            one = Send(x.at[me ^ j], o.at[me], ss.at[j], rs.at[j], at.other(j))
            one.start()
            sends.append(one)
        own = pltpu.make_async_copy(x.at[me], o.at[me], ss.at[0])
        own.start()
        for _ in range(40):
            yield
        for j in range(1, 32):
            arrived(o.at[me ^ j], ss.at[j], rs.at[j], at.other(j))
        for one in sends:
            one.sent()
        own.wait()


class Chain:
    @staticmethod
    def scratch(rows, width, kind):
        dma = pltpu.SemaphoreType.DMA
        return [
            pltpu.VMEM((4, rows, width), kind),
            pltpu.VMEM((5, rows, width), kind),
            pltpu.VMEM((rows, width), jnp.float32),
            dma((4, PIECES)),
            dma((4, PIECES)),
            dma((4, PIECES)),
            dma((5, PIECES)),
            dma((1,)),
        ]

    def __init__(self, at, parts, out, scratch, order):
        self.at, self.parts, self.out, self.order = at, parts, out, order
        self.side, self.inflow, self.total, self.ysend, self.yrecv, self.zsend, self.zrecv, self.osem = scratch
        self.rows = parts.shape[1] // PIECES

    def cut(self, p):
        return pl.ds(pl.multiple_of(p * self.rows, self.rows), self.rows)

    def side_copy(self, t, p):
        at = self.at
        return Send(
            self.parts.at[2 * t + 1 - at.y, self.cut(p)], self.side.at[t, self.cut(p)], self.ysend.at[t, p], self.yrecv.at[t, p], at.beside
        )

    def send_side(self, t):
        for p in range(PIECES):
            self.side_copy(t, p).start()

    def z_copy(self, t, p, rising):
        at = self.at
        slot = t if rising else jnp.where(t == at.z - 1, 4, t)
        mine = self.parts.at[2 * t + at.y, self.cut(p)]
        target = (None, (at.up if rising else at.down)[1])
        return Send(mine, self.inflow.at[slot, self.cut(p)], self.zsend.at[t, p], self.zrecv.at[slot, p], target)

    def wait_side(self, t, p):
        arrived(self.side.at[t, self.cut(p)], self.ysend.at[t, p], self.yrecv.at[t, p], self.at.beside)

    def wait_inflow(self, slot, p):
        arrived(self.inflow.at[slot, self.cut(p)], self.zsend.at[0, p], self.zrecv.at[slot, p], self.at.down)

    def step(self, k, p):
        at = self.at
        group = 16
        rises, falls = self.order(k)
        for t, cond, rising in ((rises, at.z < rises, True), (falls, at.z > falls, False)):

            @pl.when(cond)
            def _():
                self.wait_side(t, p)
                first = at.z == (0 if rising else 3)

                def add(inner):
                    def one(i, _):
                        here = pl.ds(pl.multiple_of(p * self.rows + i * group, group), group)
                        value = self.parts[2 * t + at.y, here, :].astype(jnp.float32) + self.side[t, here, :].astype(jnp.float32)
                        if inner:
                            value = value + self.inflow[t, here, :].astype(jnp.float32)
                        self.parts[2 * t + at.y, here, :] = value.astype(self.parts.dtype)
                        return 0

                    lax.fori_loop(0, self.rows // group, one, 0)

                pl.when(first)(lambda: add(False))

                @pl.when(jnp.logical_not(first))
                def _():
                    self.wait_inflow(t, p)
                    add(True)

                self.z_copy(t, p, rising).start()

    def last(self, p):
        at = self.at
        group = 16
        self.wait_side(at.z, p)
        pl.when(at.z > 0)(lambda: self.wait_inflow(at.z, p))
        pl.when(at.z < 3)(lambda: self.wait_inflow(4, p))

        def one(i, _):
            here = pl.ds(pl.multiple_of(p * self.rows + i * group, group), group)
            self.total[here, :] = self.parts[at.s, here, :].astype(jnp.float32) + self.side[at.z, here, :].astype(jnp.float32)

            @pl.when(at.z > 0)
            def _():
                self.total[here, :] += self.inflow[at.z, here, :].astype(jnp.float32)

            @pl.when(at.z < 3)
            def _():
                self.total[here, :] += self.inflow[4, here, :].astype(jnp.float32)

            return 0

        lax.fori_loop(0, self.rows // group, one, 0)

    def finish(self):
        def one(p, _):
            self.last(p)
            return 0

        lax.fori_loop(0, PIECES, one, 0)
        self.out_copy().start()

    def out_copy(self):
        return pltpu.make_async_copy(self.total, self.out, self.osem.at[0])

    def sent(self):
        def one(i, _):
            t, p = i // PIECES, lax.rem(i, PIECES)
            self.side_copy(t, p).sent()

            @pl.when(t != self.at.z)
            def _():
                self.z_copy(t, p, True).sent()

            return 0

        lax.fori_loop(0, 4 * PIECES, one, 0)
        self.out_copy().wait()


def outward(k):
    return k + 1, 2 - k


def ascending(k):
    return k + 1, k


def descending(k):
    return 3 - k, 2 - k


class Dense:
    letter = "d"
    reach = ("line",)

    def __init__(self, hidden, returned, w_gate, w_up, w_down, held):
        rows, width = hidden.shape
        wide = w_gate.shape[1]
        low = hidden.dtype
        dma = pltpu.SemaphoreType.DMA
        self.ins = [hidden, returned, w_gate, w_up, w_down, held]
        sums = jax.ShapeDtypeStruct((rows, width), jnp.float32)
        grad = jax.ShapeDtypeStruct((width, wide), low)
        self.outs = [sums, jax.ShapeDtypeStruct((8, rows, width), low), grad, grad, grad]
        tokens = pltpu.VMEM((8, rows, width), low)
        weight = pltpu.VMEM((width, wide), low)
        inner = pltpu.VMEM((8, rows, wide), low)
        self.own = [tokens, tokens, weight, weight, weight, inner, inner, inner, tokens, tokens, pltpu.VMEM(held.shape, held.dtype), dma((8,))]
        self.gather = Gather(hidden)
        self.chain = Chain.scratch(rows, width, low)
        self.scratch = self.own + self.gather.scratch + self.chain

    def steps(self, at, ins, outs, scratch):
        hidden, returned, w_gate, w_up, w_down, held = ins
        count = len(self.own)
        toks, cots, wg, wu, wd, act, ggrad, ugrad, hpart, rpart, mask, sems = scratch[:count]
        scratch = scratch[count:]
        gsems, scratch = scratch[: len(self.gather.scratch)], scratch[len(self.gather.scratch) :]
        hchain = Chain(at, hpart, outs[0], scratch, outward)
        rows, width = hidden.shape
        wide = w_gate.shape[1]
        tile = 256
        loads = [
            pltpu.make_async_copy(src, dst, sems.at[i])
            for i, (src, dst) in enumerate(((w_gate, wg), (w_up, wu), (w_down, wd), (returned, cots), (held, mask)))
        ]
        relay = Relay(at, hidden, toks, gsems)
        relay.begin()
        for load in loads:
            load.start()
        yield
        for p in range(PIECES):
            relay.step(1, p)
        for load in loads:
            load.wait()
        relay.own_copy().wait()
        last_dot = lambda a, b: lax.dot_general(a, b, CONTRACT_LAST, preferred_element_type=jnp.float32)
        rows_dot = lambda a, b: lax.dot_general(a, b, CONTRACT_ROWS, preferred_element_type=jnp.float32)

        def pair(i, _):
            far = at.z < 2
            t = jnp.where(
                i == 0, at.z, jnp.where(i == 1, at.z ^ 1, jnp.where(i == 2, jnp.where(far, 2, 1), jnp.where(far, 3, 0)))
            )
            relay.wait_beside(t)
            both = pl.ds(2 * t, 2)

            def first(n, _):
                lanes = pl.ds(pl.multiple_of(n * tile, tile), tile)
                h = toks[both].reshape(2 * rows, width)
                c = cots[both].reshape(2 * rows, width)
                pre = jnp.dot(h, wg[:, lanes], preferred_element_type=jnp.float32)
                up = jnp.dot(h, wu[:, lanes], preferred_element_type=jnp.float32)
                grad = jnp.dot(c, wd[:, lanes], preferred_element_type=jnp.float32)
                value, slope = gelu_parts(pre)
                keep = mask[0:1, lanes]
                put = lambda ref, v: ref.__setitem__((both, slice(None), lanes), v.astype(ref.dtype).reshape(2, rows, tile))
                put(act, value * up * keep)
                put(ggrad, grad * up * slope * keep)
                put(ugrad, grad * value * keep)
                pl.when(n == 1)(lambda: relay.step(i + 2, 0))
                pl.when(n == 3)(lambda: relay.step(i + 2, 1))
                return 0

            lax.fori_loop(0, wide // tile, first, 0)

            def second(n, _):
                lanes = pl.ds(pl.multiple_of(n * tile, tile), tile)
                a = act[both].reshape(2 * rows, wide)
                g = ggrad[both].reshape(2 * rows, wide)
                u = ugrad[both].reshape(2 * rows, wide)
                put = lambda ref, v: ref.__setitem__((both, slice(None), lanes), v.astype(ref.dtype).reshape(2, rows, tile))
                put(hpart, last_dot(g, wg[lanes, :]) + last_dot(u, wu[lanes, :]))
                put(rpart, last_dot(a, wd[lanes, :]))
                pl.when(n == 2)(lambda: relay.step(i + 2, 2))
                pl.when(n == 6)(lambda: relay.step(i + 2, 3))
                return 0

            lax.fori_loop(0, width // tile, second, 0)
            hchain.send_side(t)
            return 0

        lax.fori_loop(0, 4, pair, 0)
        out = pltpu.make_async_copy(rpart, outs[1], sems.at[7])
        out.start()

        def grads(r):
            lanes = pl.ds(pl.multiple_of(r * tile, tile), tile)
            h = toks[:, :, lanes].reshape(8 * rows, tile)
            c = cots[:, :, lanes].reshape(8 * rows, tile)
            wg[lanes, :] = rows_dot(h, ggrad[...].reshape(8 * rows, wide)).astype(wg.dtype)
            wu[lanes, :] = rows_dot(h, ugrad[...].reshape(8 * rows, wide)).astype(wu.dtype)
            wd[lanes, :] = rows_dot(c, act[...].reshape(8 * rows, wide)).astype(wd.dtype)

        def hstep(i, _):
            hchain.step(i // PIECES, lax.rem(i, PIECES))
            pl.when(i < width // tile)(lambda: grads(i))
            return 0

        lax.fori_loop(0, 3 * PIECES, hstep, 0)
        hchain.finish()
        stores = [pltpu.make_async_copy(src, dst, sems.at[i]) for i, (src, dst) in enumerate(((wg, outs[2]), (wu, outs[3]), (wd, outs[4])))]
        for store in stores:
            store.start()
        hchain.sent()
        relay.sent()
        for store in stores + [out]:
            store.wait()
        yield


class Relay:
    def __init__(self, at, x, o, sems):
        self.at, self.x, self.o = at, x, o
        self.own_sem, self.recv, self.ups, self.downs, self.sides = sems
        self.rows = x.shape[0] // PIECES

    def cut(self, p):
        return pl.ds(p * self.rows, self.rows)

    def copy(self, src, block, p, sem, target):
        return Send(src, self.o.at[block, self.cut(p)], sem, self.recv.at[block, p], target)

    def own_copy(self):
        return pltpu.make_async_copy(self.x, self.o.at[self.at.s], self.own_sem.at[0])

    def begin(self):
        at = self.at
        self.own_copy().start()
        for p in range(PIECES):
            src = self.x.at[self.cut(p)]
            self.copy(src, at.s, p, self.ups.at[0, p], at.up).start()
            self.copy(src, at.s, p, self.downs.at[0, p], at.down).start()
            self.copy(src, at.s, p, self.sides.at[0, p], at.beside).start()

    def halves(self, d):
        at = self.at
        low = (at.z >= d, jnp.maximum(at.s - 2 * d, 0), self.ups, at.up, d, at.down)
        high = (at.z + d <= 3, jnp.minimum(at.s + 2 * d, 7), self.downs, at.down, 3 + d, at.up)
        return low, high

    def step(self, d, p):
        for cond, block, along, ahead, slot, source in self.halves(d):

            @pl.when(cond)
            def _():
                here = self.o.at[block, self.cut(p)]
                arrived(here, self.ups.at[0, p], self.recv.at[block, p], source)
                self.copy(here, block, p, along.at[d, p], ahead).start()
                self.copy(here, block, p, self.sides.at[slot, p], self.at.beside).start()

    def wait_beside(self, t):
        block = 2 * t + 1 - self.at.y
        for p in range(PIECES):
            arrived(self.o.at[block, self.cut(p)], self.ups.at[0, p], self.recv.at[block, p], self.at.beside)

    def sent(self):
        at = self.at
        for p in range(PIECES):
            src = self.x.at[self.cut(p)]
            self.copy(src, at.s, p, self.ups.at[0, p], at.up).sent()
            self.copy(src, at.s, p, self.downs.at[0, p], at.down).sent()
            self.copy(src, at.s, p, self.sides.at[0, p], at.beside).sent()
            for d in range(1, 4):
                for cond, block, along, ahead, slot, source in self.halves(d):

                    @pl.when(cond)
                    def _():
                        here = self.o.at[block, self.cut(p)]
                        self.copy(here, block, p, along.at[d, p], ahead).sent()
                        self.copy(here, block, p, self.sides.at[slot, p], at.beside).sent()


def exchange(jobs, collective, name, plan=()):
    def kernel(*refs):
        at = Spot()
        refs = list(refs)
        take = lambda count: [refs.pop(0) for _ in range(count)]
        ins = [take(len(job.ins)) for job in jobs]
        outs = [take(len(job.outs)) for job in jobs]
        scratch = [take(len(job.scratch)) for job in jobs]
        at.meet({one for job in jobs for one in job.reach})
        running = [job.steps(at, i, o, s) for job, i, o, s in zip(jobs, ins, outs, scratch)]
        turns = iter(plan)
        while running:
            if plan and running[0] is not None:
                if next(running[0], plan) is plan:
                    running[0] = None
                for letter in next(turns, ""):
                    for job, one in zip(jobs, running):
                        if one is not None and job.letter == letter:
                            next(one, None)
            else:
                running = [one for one in running if one is not None and next(one, running) is not running]

    count = sum(len(job.ins) for job in jobs)
    return pl.pallas_call(
        kernel,
        out_shape=[shape for job in jobs for shape in job.outs],
        in_specs=[pl.BlockSpec(memory_space=pl.ANY)] * count,
        out_specs=[pl.BlockSpec(memory_space=pl.ANY)] * sum(len(job.outs) for job in jobs),
        scratch_shapes=[shape for job in jobs for shape in job.scratch],
        compiler_params=pltpu.CompilerParams(
            collective_id=collective, has_side_effects=True, vmem_limit_bytes=62 * 2**20
        ),
        name=name,
    )(*[x for job in jobs for x in job.ins])


class Rows:
    letter = "o"

    def __init__(self, x, near):
        self.slots = 3 if near else 1
        self.reach = ("seq", "pair") if near else ("pair",)
        self.ins = [x]
        self.outs = [jax.ShapeDtypeStruct((self.slots, 4) + x.shape, x.dtype)]
        dma = pltpu.SemaphoreType.DMA
        self.scratch = [dma((3,))] * 4 + [dma((3, 2))] * 2

    def places(self, at):
        after = (None, (lax.rem(at.s + 1, 8), at.f))
        before = (None, (lax.rem(at.s + 7, 8), at.f))
        return after, before

    def steps(self, at, ins, outs, scratch):
        (x,), (o,) = ins, outs
        asend, arecv, xsend, xrecv, csend, crecv = scratch
        after, before = self.places(at)
        sends = []

        def send(src, dst, ss, rs, target):
            one = Send(src, dst, ss, rs, target)
            one.start()
            sends.append(one)

        middle = self.slots // 2
        if self.slots == 3:
            send(x, o.at[0, at.f], asend.at[0], arecv.at[0], after)
            send(x, o.at[2, at.f], asend.at[2], arecv.at[2], before)
        own = pltpu.make_async_copy(x, o.at[middle, at.f], asend.at[1])
        own.start()
        send(x, o.at[middle, at.f], xsend.at[middle], xrecv.at[middle], at.across)
        send(x, o.at[middle, at.f], csend.at[middle, 0], crecv.at[middle, 0], at.twin)
        yield
        for j in range(self.slots):
            if j != middle:
                here = o.at[j, at.f]
                arrived(here, asend.at[j], arecv.at[j], before if j == 0 else after)
                send(here, here, xsend.at[j], xrecv.at[j], at.across)
                send(here, here, csend.at[j, 0], crecv.at[j, 0], at.twin)
        yield
        for j in range(self.slots):
            there = o.at[j, at.f ^ 2]
            arrived(there, xsend.at[j], xrecv.at[j], at.across)
            send(there, there, csend.at[j, 1], crecv.at[j, 1], at.twin)
            yield
        for j in range(self.slots):
            for k in range(2):
                arrived(o.at[j, (at.f ^ 1) ^ (2 * k)], csend.at[j, k], crecv.at[j, k], at.twin)
        for one in sends:
            one.sent()
        own.wait()


def rms_rows(values):
    mean = jnp.mean(values * values, axis=1, keepdims=True) + EPSILON
    guess = lax.rsqrt(mean)
    return guess * (1.5 - 0.5 * mean * guess * guess)


class MixerForward:
    letter = "m"
    reach = ("line",)

    def __init__(self, x_full, w_branch, w_input, w_out, igate, dgate, gain, mask, taps, soft):
        _, rows, width = x_full.shape
        window, head = igate.shape
        tokens = 8 * rows
        low, full = x_full.dtype, jnp.float32
        dma = pltpu.SemaphoreType.DMA
        self.ins = [x_full, w_branch, w_input, w_out, igate, dgate, gain, mask, taps, soft]
        kinds = [low, full, low, low, full, full, full, low]
        shapes = [(8, rows, width)] + [(tokens, window)] * 7
        self.outs = [jax.ShapeDtypeStruct((rows, width), full)]
        self.outs += [jax.ShapeDtypeStruct(shape, kind) for shape, kind in zip(shapes, kinds)]
        self.kept = [pltpu.VMEM(shape, kind) for shape, kind in zip(shapes, kinds)]
        self.held = [pltpu.VMEM(x.shape, x.dtype) for x in self.ins[1:]]
        self.local = [
            pltpu.VMEM((8, rows, width), low),
            pltpu.VMEM((8 + 2 * rows, window), full),
            pltpu.VMEM((CHUNK, head), full),
            pltpu.VMEM((CHUNK, head), full),
            pltpu.VMEM((8, window), full),
            dma((len(self.ins),)),
            dma((len(kinds),)),
        ]
        self.chain = Chain.scratch(rows, width, low)
        self.scratch = self.kept + self.held + self.local + self.chain

    def steps(self, at, ins, outs, scratch):
        take = lambda count: [scratch.pop(0) for _ in range(count)]
        scratch = list(scratch)
        kept = take(len(self.kept))
        held = take(len(self.held))
        parts, padded, coef, drive, carry, lsem, ssem = take(len(self.local))
        normed, pre, conv_in, rounded, gin, gdec, states, mixed = kept
        w_branch, w_input, w_out, igate, dgate, gain, mask, taps, soft = held
        chain = Chain(at, parts, outs[0], scratch, ascending)
        _, rows, width = normed.shape
        window, head = igate.shape
        span = 2 * rows
        loads = [pltpu.make_async_copy(src, dst, lsem.at[i]) for i, (src, dst) in enumerate(zip(ins, [normed] + held))]
        for load in loads:
            load.start()
        yield
        for load in loads:
            load.wait()
        padded[0:8, :] = jnp.zeros((8, window), jnp.float32)
        carry[...] = jnp.zeros_like(carry)
        line = lax.broadcasted_iota(jnp.int32, (8, head), 0)

        def scale(i, _):
            block, here = i // (rows // 16), pl.ds(pl.multiple_of(lax.rem(i, rows // 16) * 16, 16), 16)
            value = normed[block, here, :].astype(jnp.float32)
            normed[block, here, :] = (value * rms_rows(value) * gain[0:1, :]).astype(normed.dtype)
            return 0

        def work(t):
            lax.fori_loop(2 * t * (rows // 16), 2 * (t + 1) * (rows // 16), scale, 0)
            tokens = pl.ds(span * t, span)
            source = normed[2 * t : 2 * t + 2].reshape(span, width)
            if t:
                padded[0:8, :] = padded[span : span + 8, :]
            for h in range(window // head):
                lanes = slice(h * head, (h + 1) * head)
                pre[tokens, lanes] = jnp.dot(source, w_branch[:, lanes], preferred_element_type=jnp.float32)
                value = jnp.dot(source, w_input[:, lanes], preferred_element_type=jnp.float32).astype(conv_in.dtype)
                conv_in[tokens, lanes] = value
                padded[8:, lanes] = value.astype(jnp.float32)
            if t:
                yield

            def piece(c, _):
                for h in range(window // head):
                    lanes = slice(h * head, (h + 1) * head)
                    base = pl.multiple_of(c * CHUNK, CHUNK)
                    here = pl.ds(pl.multiple_of(t * span + base, CHUNK), CHUNK)
                    marks = mask[here, :]
                    rolls = padded[pl.ds(base, CHUNK + 8), lanes]
                    out = taps[0:1, lanes] * rolls[8:]
                    for k in range(1, TAPS):
                        out = out + taps[k : k + 1, lanes] * rolls[8 - k : 8 - k + CHUNK] * marks[:, k : k + 1]
                    small = out.astype(rounded.dtype)
                    rounded[here, lanes] = small
                    g_in = jax.nn.sigmoid(jnp.dot(small, igate[lanes, :], preferred_element_type=jnp.float32))
                    g_dec = jax.nn.sigmoid(jnp.dot(small, dgate[lanes, :], preferred_element_type=jnp.float32))
                    gin[here, lanes] = g_in
                    gdec[here, lanes] = g_dec
                    log_decay = -soft[0:1, lanes] * (1.0 + 7.0 * g_dec)
                    root = jnp.sqrt(minus_expm1(2.0 * log_decay))
                    restart = marks[:, 0:1]
                    carried = 1.0 - restart
                    coef[...] = jnp.exp(log_decay) * carried
                    drive[...] = small.astype(jnp.float32) * g_in * (restart + carried * root)

                    def tile(i, state):
                        now = pl.multiple_of(i * 8, 8)
                        a = coef[pl.ds(now, 8), :]
                        b = drive[pl.ds(now, 8), :]
                        for sh in (1, 2, 4):
                            keep = line >= sh
                            b = b + a * jnp.where(keep, pltpu.roll(b, sh, 0), 0.0)
                            a = a * jnp.where(keep, pltpu.roll(a, sh, 0), 1.0)
                        new = b + a * state
                        there = pl.ds(pl.multiple_of(t * span + base + now, 8), 8)
                        states[there, lanes] = new
                        return jnp.broadcast_to(new[7:8, :], (8, head))

                    carry[:, lanes] = lax.fori_loop(0, CHUNK // 8, tile, carry[:, lanes], unroll=True)
                    branch, _ = gelu_parts(pre[here, lanes])
                    mixed[here, lanes] = (states[here, lanes] * branch).astype(mixed.dtype)
                return 0

            lax.fori_loop(0, span // CHUNK, piece, 0)
            if t:
                yield
            values = mixed[tokens, :]

            def product(n, _):
                columns = pl.ds(pl.multiple_of(n * 256, 256), 256)
                out = jnp.dot(values, w_out[:, columns], preferred_element_type=jnp.float32)
                parts[2 * t : 2 * t + 2, :, columns] = out.astype(parts.dtype).reshape(2, rows, 256)
                return 0

            lax.fori_loop(0, width // 256, product, 0)
            chain.send_side(t)

        for t in range(4):
            yield from work(t)
            yield
        stores = [pltpu.make_async_copy(src, dst, ssem.at[i]) for i, (src, dst) in enumerate(zip(kept, outs[1:]))]
        for store in stores:
            store.start()
        for k in range(3):
            for p in range(PIECES):
                chain.step(k, p)
                yield
        chain.finish()
        yield
        chain.sent()
        for store in stores:
            store.wait()


class MixerBackward:
    letter = "b"
    reach = ("line",)

    def __init__(self, out_grad, w_out, w_branch, w_input, normed, pre, conv_in, rounded, gin, gdec, states, mixed, igate, dgate, mask, ahead, taps, soft, owned):
        rows, width = out_grad.shape
        tokens, window = pre.shape
        head = igate.shape[1]
        low, full = out_grad.dtype, jnp.float32
        dma = pltpu.SemaphoreType.DMA
        self.ins = [out_grad, w_out, w_branch, w_input, normed, pre, conv_in, rounded, gin, gdec, states, mixed, igate, dgate, mask, ahead, taps, soft, owned]
        shape = jax.ShapeDtypeStruct
        self.outs = [
            shape((rows, width), full), shape((width, window), low), shape((width, window), low), shape((window, width), low),
            shape((window, head), full), shape((window, head), full), shape((8, window), full),
        ]
        self.held = [pltpu.VMEM(x.shape, x.dtype) for x in self.ins[1:]]
        self.held[9] = pltpu.VMEM((8 + tokens, window), full)
        self.local = [
            pltpu.VMEM((8, rows, width), low),
            pltpu.VMEM((8, rows, width), low),
            pltpu.VMEM((2 * rows, window), full),
            pltpu.VMEM((tokens, window), low),
            pltpu.VMEM((tokens, window), low),
            pltpu.VMEM((2 * rows + 8, window), full),
            pltpu.VMEM((2 * rows + 8, window), full),
            pltpu.VMEM((CHUNK, head), full),
            pltpu.VMEM((CHUNK, head), full),
            pltpu.VMEM((16, window), full),
            pltpu.VMEM((window, head), full),
            pltpu.VMEM((window, head), full),
            pltpu.VMEM((8 * 5, window), full),
            pltpu.VMEM((8, window), full),
            dma((len(self.ins),)),
            dma((8,)),
        ]
        self.gather = Gather(out_grad)
        self.chain = Chain.scratch(rows, width, low)
        self.scratch = self.held + self.local + self.gather.scratch + self.chain

    def steps(self, at, ins, outs, scratch):
        scratch = list(scratch)
        take = lambda count: [scratch.pop(0) for _ in range(count)]
        held = take(len(self.held))
        toks, parts, mgrad, pgrad, cgrad, padded, later, coef, drive, carry, igrad, dgrad, sums, lines, lsem, ssem = take(len(self.local))
        gsems = take(len(self.gather.scratch))
        w_out, w_branch, w_input, normed, pre, conv_in, rounded, gin, gdec, states, mixed, igate, dgate, mask, ahead, taps, soft, owned = held
        chain = Chain(at, parts, outs[0], scratch, descending)
        relay = Relay(at, ins[0], toks, gsems)
        _, rows, width = toks.shape
        tokens, window = pre.shape
        head = igate.shape[1]
        span = 2 * rows
        heads = [slice(h * head, (h + 1) * head) for h in range(window // head)]
        relay.begin()
        loads = []
        for i, (src, dst) in enumerate(zip(ins[1:], held)):
            loads.append(pltpu.make_async_copy(src, dst.at[8:] if dst is states else dst, lsem.at[i]))
            loads[-1].start()
        states[0:8, :] = jnp.zeros((8, window), jnp.float32)
        for ref in (later, carry, igrad, dgrad, sums):
            ref[...] = jnp.zeros_like(ref)
        yield
        for d in range(1, 4):
            for p in range(PIECES):
                relay.step(d, p)
                yield
        for load in loads:
            load.wait()
        relay.own_copy().wait()
        for t in range(4):
            relay.wait_beside(t)
        line = lax.broadcasted_iota(jnp.int32, (8, head), 0)
        rows_dot = lambda a, b: lax.dot_general(a, b, CONTRACT_ROWS, preferred_element_type=jnp.float32)
        last_dot = lambda a, b: lax.dot_general(a, b, CONTRACT_LAST, preferred_element_type=jnp.float32)
        fold = lambda v: jnp.sum(v.reshape(v.shape[0] // 8, 8, v.shape[1]), axis=0)

        def work(t):
            source = toks[2 * t : 2 * t + 2].reshape(span, width)
            for lanes in heads:
                mgrad[:, lanes] = last_dot(source, w_out[lanes, :])
            later[span : span + 8, :] = later[0:8, :]
            if t:
                padded[0:8, :] = conv_in[span * t - 16 : span * t, :].astype(jnp.float32)[8:]
            else:
                padded[0:8, :] = jnp.zeros((8, window), jnp.float32)
            padded[8:, :] = conv_in[span * t : span * (t + 1), :].astype(jnp.float32)

            def piece(step, _):
                base = pl.multiple_of((span // CHUNK - 1 - step) * CHUNK, CHUNK)
                here = pl.ds(pl.multiple_of(t * span + base, CHUNK), CHUNK)
                inside = pl.ds(base, CHUNK)
                marks = mask[here, :]
                restart = marks[:, 0:1]
                carried = 1.0 - restart
                for lanes in heads:
                    branch, slope = gelu_parts(pre[here, lanes])
                    grad = mgrad[inside, lanes]
                    state = states[pl.ds(pl.multiple_of(t * span + base, CHUNK), CHUNK + 8), lanes]
                    pgrad[here, lanes] = (grad * state[8:] * slope * owned[0:1, lanes]).astype(pgrad.dtype)
                    g_dec = gdec[here, lanes]
                    g_in = gin[here, lanes]
                    log_decay = -soft[0:1, lanes] * (1.0 + 7.0 * g_dec)
                    decays = jnp.exp(log_decay)
                    root = jnp.sqrt(minus_expm1(2.0 * log_decay))
                    coef[...] = decays * carried
                    drive[...] = grad * branch

                    def tile(i, pair):
                        adj_next, coef_next = pair
                        now = pl.multiple_of(CHUNK - 8 - i * 8, 8)
                        first = coef[pl.ds(now, 8), :]
                        a = jnp.where(line == 7, coef_next, pltpu.roll(first, 7, 0))
                        b = drive[pl.ds(now, 8), :]
                        for sh in (1, 2, 4):
                            keep = line < 8 - sh
                            b = b + a * jnp.where(keep, pltpu.roll(b, 8 - sh, 0), 0.0)
                            a = a * jnp.where(keep, pltpu.roll(a, 8 - sh, 0), 1.0)
                        new = b + a * adj_next
                        drive[pl.ds(now, 8), :] = new
                        return jnp.broadcast_to(new[0:1, :], (8, head)), jnp.broadcast_to(first[0:1, :], (8, head))

                    adj_next, coef_next = lax.fori_loop(0, CHUNK // 8, tile, (carry[0:8, lanes], carry[8:16, lanes]), unroll=True)
                    carry[0:8, lanes] = adj_next
                    carry[8:16, lanes] = coef_next
                    adjoint = drive[...]
                    small = rounded[here, lanes]
                    value = small.astype(jnp.float32)
                    log_grad = adjoint * carried * decays * (state[7 : 7 + CHUNK] - value * g_in * decays / root)
                    sums[32:40, lanes] += fold(-log_grad * (1.0 + 7.0 * g_dec))
                    through = adjoint * g_in * (restart + carried * root)
                    ipg = (through * value * (1.0 - g_in)).astype(jnp.bfloat16)
                    dpg = (log_grad * (-7.0 * soft[0:1, lanes]) * g_dec * (1.0 - g_dec)).astype(jnp.bfloat16)
                    igrad[lanes, :] += rows_dot(small, ipg)
                    dgrad[lanes, :] += rows_dot(small, dpg)
                    through = through + last_dot(ipg, igate[lanes, :]) + last_dot(dpg, dgate[lanes, :])
                    later[inside, lanes] = through.astype(jnp.bfloat16).astype(jnp.float32)
                return 0

            lax.fori_loop(0, span // CHUNK, piece, 0)
            yield

            def after(c, _):
                base = pl.multiple_of(c * CHUNK, CHUNK)
                here = pl.ds(pl.multiple_of(t * span + base, CHUNK), CHUNK)
                marks = mask[here, :]
                ahead_marks = ahead[here, :]
                for lanes in heads:
                    follow = later[pl.ds(base, CHUNK + 8), lanes]
                    before = padded[pl.ds(base, CHUNK + 8), lanes]
                    grad = follow[:CHUNK]
                    total = taps[0:1, lanes] * grad
                    sums[0:8, lanes] += fold(grad * before[8:])
                    for k in range(1, TAPS):
                        total = total + taps[k : k + 1, lanes] * follow[k : k + CHUNK] * ahead_marks[:, k : k + 1]
                        sums[8 * k : 8 * k + 8, lanes] += fold(grad * before[8 - k : 8 - k + CHUNK] * marks[:, k : k + 1])
                    cgrad[here, lanes] = (total * owned[0:1, lanes]).astype(cgrad.dtype)
                return 0

            lax.fori_loop(0, span // CHUNK, after, 0)
            mine = slice(span * t, span * (t + 1))

            def product(n, _):
                columns = pl.ds(pl.multiple_of(n * 256, 256), 256)
                out = last_dot(pgrad[mine, :], w_branch[columns, :]) + last_dot(cgrad[mine, :], w_input[columns, :])
                parts[2 * t : 2 * t + 2, :, columns] = out.astype(parts.dtype).reshape(2, rows, 256)
                return 0

            lax.fori_loop(0, width // 256, product, 0)
            chain.send_side(t)

        for t in (3, 2, 1, 0):
            yield from work(t)
            yield
        for k in range(5):
            lines[k : k + 1, :] = jnp.sum(sums[8 * k : 8 * k + 8, :], axis=0, keepdims=True)
        lines[5:8, :] = jnp.zeros((3, window), jnp.float32)

        def grads(r):
            lanes = pl.ds(pl.multiple_of(r * 256, 256), 256)
            value = normed[:, :, lanes].reshape(tokens, 256)
            w_branch[lanes, :] = rows_dot(value, pgrad[...]).astype(w_branch.dtype)
            w_input[lanes, :] = rows_dot(value, cgrad[...]).astype(w_input.dtype)
            w_out[:, lanes] = rows_dot(mixed[...], toks[:, :, lanes].reshape(tokens, 256)).astype(w_out.dtype)

        done = 0
        for k in range(3):

            def chain_step(p, _):
                chain.step(k, p)
                pl.when(k * PIECES + p < width // 256)(lambda: grads(k * PIECES + p))
                return 0

            lax.fori_loop(0, PIECES, chain_step, 0)
            yield
        chain.finish()
        stores = [
            pltpu.make_async_copy(src, dst, ssem.at[i])
            for i, (src, dst) in enumerate(zip((w_branch, w_input, w_out, igrad, dgrad, lines), outs[1:]))
        ]
        for store in stores:
            store.start()
        yield
        chain.sent()
        relay.sent()
        for store in stores:
            store.wait()


def fast(
    inputs,
    resets,
    cotangent,
    first_gain,
    branch_weight,
    input_weight,
    conv_weight,
    input_gate,
    decay_gate,
    decay_param,
    output_weight,
    second_gain,
    gate_weight,
    up_weight,
    down_weight,
):
    low = jnp.bfloat16
    peers, groups = 8, 4
    s, f = lax.axis_index("seq"), lax.axis_index("fsdp")
    sources_low = inputs[0]
    sources = sources_low.astype(jnp.float32)
    returned = cotangent[0]
    tokens, width = sources.shape
    rows = branch_weight.shape[0]
    head = input_gate.shape[1]
    own = width // peers
    hidden_own = gate_weight.shape[1] // peers
    all_tokens = peers * tokens
    firsts = [min(own * at // head, width // head - 2) for at in range(peers)]
    window = 2 * head
    offset = own * s - head * jnp.minimum(own * s // head, width // head - 2)
    owned = ((jnp.arange(window) >= offset) & (jnp.arange(window) < offset + own)).astype(jnp.float32)

    small = jnp.zeros((8, 128), jnp.float32)
    small = small.at[0, :rows].set(first_gain.astype(jnp.float32))
    small = small.at[1, :rows].set(second_gain.astype(jnp.float32))
    small = small.at[2, :tokens].set(resets[0].astype(jnp.float32))
    small = jnp.broadcast_to(small[None], (peers * groups, 8, 128))
    mixer_start = lambda to: head * jnp.minimum(own * to // head, width // head - 2)
    dense_start = lambda to: 128 * (hidden_own * to // 128)
    wide = 128 * -(-hidden_own // 128)
    lanes = jnp.arange(wide) + dense_start(s) - hidden_own * s
    held = jnp.broadcast_to(((lanes >= 0) & (lanes < hidden_own)).astype(jnp.float32)[None], (8, wide))
    pad = jnp.zeros((rows, 128 - 5), low)
    row_pack = jnp.concatenate([input_gate, decay_gate, conv_weight, decay_param[:, None], pad], axis=1)
    x_full, w_branch, w_input, row_w, out_w, vectors = exchange(
        [
            Gather(sources_low),
            Spread(branch_weight, mixer_start, window),
            Spread(input_weight, mixer_start, window),
            Rows(row_pack, True),
            Rows(output_weight, False),
            Tiny(small),
        ],
        1,
        "first_exchange",
    )
    whole = lambda w: w.reshape(width, w.shape[-1])
    w_branch, w_input = whole(w_branch), whole(w_input)
    w_output = out_w.reshape(own, width)
    before = jnp.concatenate(
        [
            lax.ppermute(w_output[own - 192 :], "seq", [(i, i + 1) for i in range(peers - 1)]),
            w_output,
            lax.ppermute(w_output[:192], "seq", [(i + 1, i) for i in range(peers - 1)]),
        ]
    )
    w_output_window = lax.dynamic_slice_in_dim(before, 192 - offset, window, 0)
    w_output_own = lax.dynamic_update_slice_in_dim(jnp.zeros((window, width), low), w_output, offset, 0)
    near = lax.dynamic_slice_in_dim(row_w.reshape(3 * own, row_pack.shape[1]), own - offset, window, 0)
    w_igate, w_dgate = near[:, :head], near[:, head : 2 * head]
    taps = jnp.zeros((8, window), jnp.float32).at[:4].set(near[:, 2 * head : 2 * head + 4].astype(jnp.float32).T)
    w_decay = near[:, 2 * head + 4].astype(jnp.float32)
    soft = jnp.broadcast_to(jax.nn.softplus(w_decay)[None], (8, window))
    gain_first = vectors[:, 0, :rows].reshape(width)
    gain_second = vectors[:, 1, :rows].reshape(width)
    flags = lax.dynamic_index_in_dim(vectors.reshape(peers, groups, 8, 128), f, 1, False)[:, 2, :tokens].reshape(all_tokens)
    segment = jnp.cumsum(flags)
    masks, aheads = [flags], [jnp.ones_like(flags)]
    for k in range(1, 4):
        same = (segment[k:] == segment[:-k]).astype(jnp.float32)
        masks.append(jnp.concatenate([jnp.zeros((k,), jnp.float32), same]))
        aheads.append(jnp.concatenate([same, jnp.zeros((k,), jnp.float32)]))
    masks = jnp.stack(masks + [jnp.zeros_like(flags)] * 4, axis=1)
    aheads = jnp.stack(aheads + [jnp.zeros_like(flags)] * 4, axis=1)
    owned_rows = jnp.broadcast_to(owned[None], (8, window))

    gain_rows = jnp.broadcast_to(gain_first[None], (8, width))
    (
        mixer_out, normed, pre, conv_in, rounded, gate_in, gate_dec, states, mixed,
        returned_full, w_gate, w_up, w_down,
    ) = exchange(
        [
            MixerForward(x_full, w_branch, w_input, w_output_own, w_igate, w_dgate, gain_rows, masks, taps, soft),
            Gather(returned),
        ]
        + [Spread(w, dense_start, wide) for w in (gate_weight, up_weight, down_weight)],
        2,
        "mixer_forward",
        ["gs"] + [""] * 9 + ["ggggsssggggssggggsss"] + [""] * 12,
    )
    resid = sources + mixer_out
    scale_two = lax.rsqrt(jnp.mean(resid * resid, axis=1, keepdims=True) + EPSILON)
    hidden = (resid * scale_two * gain_second).astype(low)
    hidden_grad, result_part, grad_gate, grad_up, grad_down = exchange(
        [Dense(hidden, returned_full, whole(w_gate), whole(w_up), whole(w_down), held)], 3, "dense"
    )
    weighted = hidden_grad * gain_second
    resid_grad = (
        returned.astype(jnp.float32)
        + scale_two * weighted
        - resid * scale_two**3 * jnp.mean(weighted * resid, axis=1, keepdims=True)
    )
    second_term = jnp.sum(hidden_grad * resid * scale_two, axis=0)
    out_grad = resid_grad.astype(low)
    split = lambda g: g.reshape(peers, groups, rows, g.shape[-1])
    (
        normed_grad, grad_branch, grad_input, grad_output, igate_term, dgate_term, line_terms,
        grad_gate, grad_up, grad_down,
    ) = exchange(
        [
            MixerBackward(
                out_grad, w_output_window, w_branch, w_input, normed, pre, conv_in, rounded, gate_in, gate_dec, states, mixed,
                w_igate, w_dgate, masks, aheads, taps, soft, owned_rows,
            )
        ]
        + [Collect(split(g)) for g in (grad_gate, grad_up, grad_down)],
        4,
        "mixer_backward",
    )
    scale_one = lax.rsqrt(jnp.mean(sources * sources, axis=1, keepdims=True) + EPSILON)
    weighted = normed_grad * gain_first
    source_grad = (
        resid_grad
        + scale_one * weighted
        - sources * scale_one**3 * jnp.mean(weighted * sources, axis=1, keepdims=True)
    )
    first_term = jnp.sum(normed_grad * sources * scale_one, axis=0)
    take_rows = lambda g: lax.dynamic_slice_in_dim(g, offset, own, 0)
    grad_branch, grad_input, grad_output = split(grad_branch), split(grad_input), take_rows(grad_output)
    gates = take_rows(jnp.concatenate([igate_term, dgate_term], axis=1)).astype(low)
    lines = take_rows(jnp.concatenate([line_terms.T, jnp.zeros((window, 120), jnp.float32)], axis=1))
    vectors = jnp.zeros((peers * groups, 8, 128), jnp.float32)
    vectors = vectors.at[:, 0, :rows].set(first_term.reshape(peers * groups, rows))
    vectors = vectors.at[:, 1, :rows].set(second_term.reshape(peers * groups, rows))
    by_rows = lambda g: g.reshape(1, groups, rows, g.shape[-1])
    ffn_out, grad_branch, grad_input, grad_output, gates, lines, vectors = exchange(
        [Reduce(result_part), Collect(grad_branch), Collect(grad_input), Collect(by_rows(grad_output)), Collect(by_rows(gates)), Collect(by_rows(lines)), Tiny(vectors)],
        6,
        "mixer_collect",
    )
    result = (resid + ffn_out).astype(low)
    vectors = jnp.sum(vectors, axis=0)
    gates = gates[0].astype(jnp.float32)

    def join(g, starts):
        size = g.shape[-1]
        marks = sorted({edge for start in starts for edge in (start, start + size)})
        pieces = []
        for low_mark, high_mark in zip(marks[:-1], marks[1:]):
            terms = [
                g[at, :, low_mark - start : high_mark - start].astype(jnp.float32)
                for at, start in enumerate(starts)
                if start <= low_mark and high_mark <= start + size
            ]
            pieces.append(sum(terms[1:], terms[0]))
        return jnp.concatenate(pieces, axis=1)

    firsts = [head * first for first in firsts]
    dense_firsts = [128 * (hidden_own * at // 128) for at in range(peers)]
    return (
        result[None],
        source_grad.astype(low)[None],
        vectors[0, :rows],
        join(grad_branch, firsts),
        join(grad_input, firsts),
        lines[0, :, :4],
        gates[:, :head],
        gates[:, head:],
        lines[0, :, 4] * jax.nn.sigmoid(decay_param.astype(jnp.float32)),
        grad_output[0].astype(jnp.float32),
        vectors[1, :rows],
        join(grad_gate, dense_firsts),
        join(grad_up, dense_firsts),
        join(grad_down, dense_firsts),
    )


def solution(mesh):
    in_specs = (
        P("fsdp", "seq", None),
        P("fsdp", "seq"),
        P("fsdp", "seq", None),
        P(("seq", "fsdp")),
        P(("seq", "fsdp"), None),
        P(("seq", "fsdp"), None),
        P(("seq", "fsdp"), None),
        P(("seq", "fsdp"), None),
        P(("seq", "fsdp"), None),
        P(("seq", "fsdp")),
        P(("seq", "fsdp"), None),
        P(("seq", "fsdp")),
        P(("seq", "fsdp"), None),
        P(("seq", "fsdp"), None),
        P(("seq", "fsdp"), None),
    )
    out_specs = (
        P("fsdp", "seq", None),
        P("fsdp", "seq", None),
        P(("seq", "fsdp")),
        P(("seq", "fsdp"), None),
        P(("seq", "fsdp"), None),
        P(("seq", "fsdp"), None),
        P(("seq", "fsdp"), None),
        P(("seq", "fsdp"), None),
        P(("seq", "fsdp")),
        P(("seq", "fsdp"), None),
        P(("seq", "fsdp")),
        P(("seq", "fsdp"), None),
        P(("seq", "fsdp"), None),
        P(("seq", "fsdp"), None),
    )
    program = fast if dict(mesh.shape) == {"seq": 8, "fsdp": 4} else local
    return jax.shard_map(program, mesh=mesh, in_specs=in_specs, out_specs=out_specs, check_vma=False)
```

profile of v0, /device:TPU:8, one launch (start us, length us, event | category | flops | bytes accessed | tf_op | source)
XLA Modules:
  0.0 837.6 jit_solution(3242453589008298263)
XLA Ops:
  0.6 0.8 copy.56
  1.4 0.8 copy.57
  4.3 1.5 concatenate.58.refs_3_
  5.9 0.7 broadcast_in_dim.24.refs_5_
  6.5 94.9 %first_exchange.1 = (bf16[8,128,2560]{2,1,0:T(8,128)(2,1)}, bf16[8,4,80,512]{3,2,1,0:T(8,128)(2,1)}, bf16[8,4,80,512]{3,2,1,0:T(8,128)(2,1)}, bf16[3,4,80,640]{3...) custom-call(bf16[128,2560]{1,0:T(8,128)(2,1)} %bitcast.215, bf16[80,2560]{1,0:T(8,128)(2,1)} %refs_1_.1, ...), custom_call_target="tpu_custom_call" | custom-call | tf_op jit(solution)/shard_map/first_exchange/pallas_call | solution.py:1343
  101.4 3.0 fusion.23
  104.4 1.9 collective-permute-start
  106.3 5.0 collective-permute-start.1
  112.3 0.9 fusion.24
  114.9 1.0 copy.62.refs_7_.refs_14_
  116.4 1.5 copy-done.2
  119.2 200.7 %mixer_forward.1 = (f32[128,2560]{1,0:T(8,128)}, bf16[8,128,2560]{2,1,0:T(8,128)(2,1)}, f32[1024,512]{1,0:T(8,128)}, bf16[1024,512]{1,0:T(8,128)(2,1)}, bf16[102...) custom-call(bf16[8,128,2560]{2,1,0:T(8,128)(2,1)} %get-tuple-element, ...), custom_call_target="tpu_custom_call" | custom-call | tf_op jit(solution)/shard_map/mixer_forward/pallas_call | solution.py:1343
  319.8 2.2 multiply_reduce_fusion.2
  323.0 1.0 multiply_convert_fusion.refs_0_
  324.7 166.0 %dense.1 = (f32[128,2560]{1,0:T(8,128)}, bf16[8,128,2560]{2,1,0:T(8,128)(2,1)}, bf16[2560,1024]{1,0:T(8,128)(2,1)}, bf16[2560,1024]{1,0:T(8,128)(2,1)}, bf16[2560,1024]{1,0:T(8,128)(2,1)}) custom-call(bf16[128,2560]{1,0:T(8,128)(2,1)} %multiply_convert_fusion.refs_0_, bf16[8,128,2560]{2,1,0:T(8,128)(2,1)} %get-tuple-element.134.refs_1_, ...), custom_call_target="tpu_custom_call" | custom-call | tf_op jit(solution)/shard_map/dense/pallas_call | solution.py:1343
  490.7 1.8 multiply_reduce_fusion
  493.2 1.0 copy.66.refs_15_
  494.3 2.9 fusion.22
  497.2 4.9 fusion.1.refs_1_
  502.8 199.0 %mixer_backward.1 = (f32[128,2560]{1,0:T(8,128)}, bf16[2560,512]{1,0:T(8,128)(2,1)}, bf16[2560,512]{1,0:T(8,128)(2,1)}, bf16[512,2560]{1,0:T(8,128)(2,1)}, f32[5...) custom-call(bf16[128,2560]{1,0:T(8,128)(2,1)} %get-tuple-element.216, ...), custom_call_target="tpu_custom_call" | custom-call | tf_op jit(solution)/shard_map/mixer_backward/pallas_call | solution.py:1343
  701.8 1.7 fusion.8
  703.6 0.7 scatter.40
  704.2 2.7 constant_dynamic-slice_fusion.1
  707.0 0.8 copy.67
  707.8 2.0 scatter.41.refs_6_
  709.8 0.8 fusion.10
  710.5 102.6 %mixer_collect.1 = (f32[128,2560]{1,0:T(8,128)}, bf16[8,80,512]{2,1,0:T(8,128)(2,1)}, bf16[8,80,512]{2,1,0:T(8,128)(2,1)}, bf16[1,80,2560]{2,1,0:T(8,128)(2,1)},...) custom-call(bf16[8,128,2560]{2,1,0:T(8,128)(2,1)} %get-tuple-element.138.refs_0_, ...), custom_call_target="tpu_custom_call" | custom-call | tf_op jit(solution)/shard_map/mixer_collect/pallas_call | solution.py:1343
  813.1 0.9 slice_bitcast_fusion
  814.0 1.0 slice_reduce_fusion
  814.9 0.9 convert_dynamic-update-slice_fusion.7
  815.9 0.8 constant_dynamic-update-slice_fusion.31
  816.6 0.9 convert_dynamic-update-slice_fusion.6
  817.6 0.9 convert_dynamic-update-slice_fusion.5
  818.5 0.8 constant_dynamic-update-slice_fusion.30
  819.3 0.9 convert_dynamic-update-slice_fusion.4
  820.2 0.9 convert_dynamic-update-slice_fusion.3
  821.1 0.8 constant_dynamic-update-slice_fusion.29
  821.9 0.9 convert_dynamic-update-slice_fusion.2
  822.8 1.0 convert_dynamic-update-slice_fusion.1
  823.9 0.8 constant_dynamic-update-slice_fusion.28
  824.6 0.9 convert_dynamic-update-slice_fusion
  825.8 1.2 copy-done.17
  827.4 1.2 copy-done.18
  829.1 1.0 copy-done.19
  830.3 1.0 bitcast_convert_fusion
  831.3 1.0 fusion.11
  832.3 0.7 fusion.25
  834.8 2.6 fusion.12
  (156 shorter events, 12.4 us)
Async XLA Ops:
  101.4 10.0 %copy-start.20 = (f32[32,8,128]{2,1,0:T(8,128)S(1)}, f32[32,8,128]{2,1,0:T(8,128)}, u32[]{:S(2)}) copy-start(f32[32,8,128]{2,1,0:T(8,128)} %get-tuple-element.132) | copy-start | bytes 393220
  101.4 10.9 %copy-start.13 = (bf16[3,4,80,640]{3,2,1,0:T(8,128)(2,1)S(1)}, bf16[3,4,80,640]{3,2,1,0:T(8,128)(2,1)}, u32[]{:S(2)}) copy-start(bf16[3,4,80,640]{3,2,1,0:T(8,128)(2,1)} %get-tuple-element.131) | copy-start | bytes 3686404
  104.4 392.8 %collective-permute-start = (bf16[192,2560]{1,0:T(8,128)(2,1)}, bf16[192,2560]{1,0:T(8,128)(2,1)}, u32[]{:S(2)}, u32[]{:S(2)}) collective-permute-start(bf16[192,2560]{1,0:T(8,128)(2,1)} %get-tuple-element.221), channel_id=1, source_target_pairs={{0,4},{4,8},{8,12},{12,16},{16,20},{20,24},{24,28},{1,5},{5,9},{9,... | collective-permute-start | bytes 2949128 | tf_op jit(solution)/shard_map/ppermute | solution.py:1834
  106.3 390.9 %collective-permute-start.1 = (bf16[192,2560]{1,0:T(8,128)(2,1)}, bf16[192,2560]{1,0:T(8,128)(2,1)}, u32[]{:S(2)}, u32[]{:S(2)}) collective-permute-start(bf16[192,2560]{1,0:T(8,128)(2,1)} %get-tuple-element.220), channel_id=1, source_target_pairs={{4,0},{8,4},{12,8},{16,12},{20,16},{24,20},{28,24},{5,1},{9,5},{13... | collective-permute-start | bytes 2949128 | tf_op jit(solution)/shard_map/ppermute | solution.py:1836
  113.2 3.0 copy-start
  116.4 1.6 copy-start.2
  119.2 200.7 %copy-start.3 = (bf16[1,128,2560]{2,1,0:T(8,128)(2,1)S(1)}, bf16[1,128,2560]{2,1,0:T(8,128)(2,1)}, u32[]{:S(2)}) copy-start(bf16[1,128,2560]{2,1,0:T(8,128)(2,1)} %param.27) | copy-start | bytes 1966084
  322.5 0.5 copy-start.25
  324.7 166.0 %copy-start.26 = (f32[128]{0:T(128)S(1)}, f32[128]{0:T(128)}, u32[]{:S(2)}) copy-start(f32[128]{0:T(128)} %copy-done.25) | copy-start | bytes 1540
  490.7 1.8 copy-start.27
  490.7 2.4 copy-start.21
  490.7 3.6 copy-start.5
  490.7 3.6 copy-start.30
  494.3 2.9 copy-start.1
  701.7 5.2 copy-start.22
  703.5 6.3 copy-start.11
  703.5 6.3 copy-start.12
  813.1 12.5 %copy-start.8 = (bf16[8,80,1024]{2,1,0:T(8,128)(2,1)S(1)}, bf16[8,80,1024]{2,1,0:T(8,128)(2,1)}, u32[]{:S(2)}) copy-start(bf16[8,80,1024]{2,1,0:T(8,128)(2,1)} %get-tuple-element.166) | copy-start | bytes 3932164
  822.8 4.3 copy-start.7
  825.5 1.4 copy-start.17
  827.0 1.6 copy-start.10
  827.1 1.4 copy-start.18
  827.2 1.9 copy-start.9
  827.3 3.0 copy-start.14
  828.6 2.7 copy-start.6
  828.6 1.4 copy-start.19
  828.8 1.5 copy-start.23
  830.1 2.2 copy-start.16
  830.1 1.2 copy-start.24
  830.3 3.3 copy-start.15
  830.3 3.9 copy-start.28
  830.3 4.4 copy-start.4
  830.3 4.4 copy-start.29
where the time goes:
time: 845 us; the launch traced here: 838 us
  Pallas kernels  763 us (90%)
  other arithmetic  36.1 us (4%)
  local copies, waits for them, and re-layouts  29.7 us (4%)
    pallas_call x5, Pallas kernels, exchange(): pl.pallas_call(kernel, out_shape=[shape for job in jobs for shape in job....  763 us
  transfers between devices with their start and end apart: 2, of which 0 were waited for; matrix products, arithmetic and copies ran while one was open for 2% of the time, Pallas kernels for 44%

commit v1 on v0

--- a/solution.py
+++ b/solution.py
@@ -1,3 +1,5 @@
+import functools
+
 import jax
 import jax.numpy as jnp
 from jax import lax
@@ -842,9 +844,9 @@
     letter = "s"
     reach = ("seq", "pair")
 
-    def __init__(self, x, starts, wide):
+    def __init__(self, x, starts, wide, letter="s"):
         self.ins = [x]
-        self.starts, self.wide = starts, wide
+        self.starts, self.wide, self.letter = starts, wide, letter
         self.outs = [jax.ShapeDtypeStruct((8, 4, x.shape[0], wide), x.dtype)]
         dma = pltpu.SemaphoreType.DMA
         self.scratch = [dma((8,)), dma((8,)), dma((8,)), dma((8,)), dma((8, 2)), dma((8, 2))]
@@ -903,8 +905,10 @@
 
 class Collect:
     letter = "c"
-    def __init__(self, x):
-        blocks, _, rows, width = x.shape
+    def __init__(self, x, window=None):
+        self.window = window
+        blocks, rows, width = (1, window.rows, x.shape[1]) if window else (x.shape[0],) + x.shape[2:]
+        self.shape = (blocks, rows, width)
         self.ins = [x]
         self.blocks = blocks
         self.reach = ("seq", "pair") if blocks > 1 else ("pair",)
@@ -916,10 +920,15 @@
     def steps(self, at, ins, outs, scratch):
         (x,), (o,) = ins, outs
         stage, tnear, tfar, xin, lsem, csend, crecv, xsend, xrecv, asend, arecv = scratch
-        rows = x.shape[2]
+        rows = self.shape[1]
         many = self.blocks > 1
         spot = (lambda j: at.s ^ j) if many else (lambda j: j)
         sends = []
+
+        def part(j, whose):
+            if self.window is None:
+                return x.at[spot(j), whose]
+            return x.at[pl.ds(pl.multiple_of(self.window.offset(at.s) + rows * whose, 16), rows)]
 
         def send(src, dst, ss, rs, target):
             one = Send(src, dst, ss, rs, target)
@@ -931,11 +940,11 @@
 
         def load(i):
             j, whose = pieces[i]
-            return pltpu.make_async_copy(x.at[spot(j), whose], stage.at[i % 2], lsem.at[i % 2])
+            return pltpu.make_async_copy(part(j, whose), stage.at[i % 2], lsem.at[i % 2])
 
         for j in order:
-            send(x.at[spot(j), at.f ^ 3], tfar.at[j], csend.at[j, 0], crecv.at[j, 0], at.twin)
-            send(x.at[spot(j), at.f ^ 1], tnear.at[j], csend.at[j, 1], crecv.at[j, 1], at.twin)
+            send(part(j, at.f ^ 3), tfar.at[j], csend.at[j, 0], crecv.at[j, 0], at.twin)
+            send(part(j, at.f ^ 1), tnear.at[j], csend.at[j, 1], crecv.at[j, 1], at.twin)
         load(0).start()
         yield
         outs_done = []
@@ -971,7 +980,8 @@
     letter = "t"
     def __init__(self, x):
         self.ins = [x]
-        self.outs = [jax.ShapeDtypeStruct(x.shape, x.dtype)]
+        self.outs = [jax.ShapeDtypeStruct((32,) + x.shape[1:], x.dtype)]
+        self.same = x.shape[0] == 1
         dma = pltpu.SemaphoreType.DMA
         self.scratch = [dma((32,)), dma((32,))]
 
@@ -981,12 +991,13 @@
         (x,), (o,) = ins, outs
         ss, rs = scratch
         me = at.s * 4 + at.f
+        part = lambda to: x.at[0] if self.same else x.at[to]
         sends = []
         for j in range(1, 32):
-            one = Send(x.at[me ^ j], o.at[me], ss.at[j], rs.at[j], at.other(j))
+            one = Send(part(me ^ j), o.at[me], ss.at[j], rs.at[j], at.other(j))
             one.start()
             sends.append(one)
-        own = pltpu.make_async_copy(x.at[me], o.at[me], ss.at[0])
+        own = pltpu.make_async_copy(part(me), o.at[me], ss.at[0])
         own.start()
         for _ in range(40):
             yield
@@ -1124,15 +1135,16 @@
 
 
 def outward(k):
-    return k + 1, 2 - k
-
-
-def ascending(k):
-    return k + 1, k
+    rises = jnp.where(k == 0, 1, jnp.where(k == 1, 3, 2))
+    return rises, 3 - rises
+
+
+def farthest(k):
+    return 3 - k, k
 
 
 def descending(k):
-    return 3 - k, 2 - k
+    return 3 - k, (2, 0, 1)[k]
 
 
 class Dense:
@@ -1189,6 +1201,11 @@
                 i == 0, at.z, jnp.where(i == 1, at.z ^ 1, jnp.where(i == 2, jnp.where(far, 2, 1), jnp.where(far, 3, 0)))
             )
             relay.wait_beside(t)
+
+            @pl.when(i == 3)
+            def _():
+                hchain.send_side(at.z ^ 1)
+
             both = pl.ds(2 * t, 2)
 
             def first(n, _):
@@ -1223,10 +1240,12 @@
                 return 0
 
             lax.fori_loop(0, width // tile, second, 0)
-            hchain.send_side(t)
             return 0
 
         lax.fori_loop(0, 4, pair, 0)
+        hchain.send_side(jnp.where(at.z < 2, 3, 0))
+        hchain.send_side(jnp.where(at.z < 2, 2, 1))
+        hchain.send_side(at.z)
         out = pltpu.make_async_copy(rpart, outs[1], sems.at[7])
         out.start()
 
@@ -1294,6 +1313,41 @@
                 arrived(here, self.ups.at[0, p], self.recv.at[block, p], source)
                 self.copy(here, block, p, along.at[d, p], ahead).start()
                 self.copy(here, block, p, self.sides.at[slot, p], self.at.beside).start()
+
+    def begin_rising(self):
+        at = self.at
+        self.own_copy().start()
+        for p in range(PIECES):
+            src = self.x.at[self.cut(p)]
+            self.copy(src, at.s, p, self.ups.at[0, p], at.up).start()
+            self.copy(src, at.s, p, self.sides.at[0, p], at.beside).start()
+
+    def take(self, half, d, p):
+        cond, block, along, ahead, slot, source = half
+
+        @pl.when(cond)
+        def _():
+            here = self.o.at[block, self.cut(p)]
+            arrived(here, self.ups.at[0, p], self.recv.at[block, p], source)
+            self.copy(here, block, p, along.at[d, p], ahead).start()
+            self.copy(here, block, p, self.sides.at[slot, p], self.at.beside).start()
+
+    def step_up(self, d, p):
+        self.take(self.halves(d)[0], d, p)
+
+    def step_down(self, k, p):
+        at = self.at
+        d = jnp.maximum(3 - k - at.z, 0)
+        high = self.halves(d)[1]
+        self.take((at.z < 3 - k,) + high[1:], d, p)
+
+    def own_down(self, top):
+        at = self.at
+        for p in range(PIECES):
+
+            @pl.when(at.z == 3 if top else at.z < 3)
+            def _():
+                self.copy(self.x.at[self.cut(p)], at.s, p, self.downs.at[0, p], at.down).start()
 
     def wait_beside(self, t):
         block = 2 * t + 1 - self.at.y
@@ -1353,37 +1407,54 @@
     )(*[x for job in jobs for x in job.ins])
 
 
+class Window:
+    def __init__(self, own, head, width, rows):
+        self.own, self.head, self.heads, self.rows = own, head, width // head, rows
+        self.size = 2 * head
+
+    def first(self, s):
+        return self.head * jnp.minimum(self.own * s // self.head, self.heads - 2)
+
+    def offset(self, s):
+        return self.own * s - self.first(s)
+
+    def takes(self, s, slot, f):
+        before = self.offset(s)
+        if slot == 0:
+            return self.own - before < (f + 1) * self.rows
+        return f * self.rows < self.size - self.own - before
+
+
 class Rows:
     letter = "o"
 
-    def __init__(self, x, near):
-        self.slots = 3 if near else 1
-        self.reach = ("seq", "pair") if near else ("pair",)
+    def __init__(self, x, window=None):
+        self.window = window
+        self.slots = 1 if window is None else 3
+        self.reach = ("pair",) if window is None else ("seq", "pair")
         self.ins = [x]
         self.outs = [jax.ShapeDtypeStruct((self.slots, 4) + x.shape, x.dtype)]
         dma = pltpu.SemaphoreType.DMA
         self.scratch = [dma((3,))] * 4 + [dma((3, 2))] * 2
 
-    def places(self, at):
-        after = (None, (lax.rem(at.s + 1, 8), at.f))
-        before = (None, (lax.rem(at.s + 7, 8), at.f))
-        return after, before
-
     def steps(self, at, ins, outs, scratch):
         (x,), (o,) = ins, outs
         asend, arecv, xsend, xrecv, csend, crecv = scratch
-        after, before = self.places(at)
+        after = lax.rem(at.s + 1, 8)
+        before = lax.rem(at.s + 7, 8)
         sends = []
 
-        def send(src, dst, ss, rs, target):
-            one = Send(src, dst, ss, rs, target)
+        def send(src, dst, ss, rs, target, cond=None):
+            one = Send(src, dst, ss, rs, (cond, target[1]))
             one.start()
             sends.append(one)
 
         middle = self.slots // 2
+        takes = (lambda j, f: self.window.takes(at.s, j, f)) if self.window else None
+        holds = lambda j, f: None if j == middle else takes(j, f)
         if self.slots == 3:
-            send(x, o.at[0, at.f], asend.at[0], arecv.at[0], after)
-            send(x, o.at[2, at.f], asend.at[2], arecv.at[2], before)
+            send(x, o.at[0, at.f], asend.at[0], arecv.at[0], (None, (after, at.f)), (at.s < 7) & self.window.takes(after, 0, at.f))
+            send(x, o.at[2, at.f], asend.at[2], arecv.at[2], (None, (before, at.f)), (at.s > 0) & self.window.takes(before, 2, at.f))
         own = pltpu.make_async_copy(x, o.at[middle, at.f], asend.at[1])
         own.start()
         send(x, o.at[middle, at.f], xsend.at[middle], xrecv.at[middle], at.across)
@@ -1392,21 +1463,65 @@
         for j in range(self.slots):
             if j != middle:
                 here = o.at[j, at.f]
-                arrived(here, asend.at[j], arecv.at[j], before if j == 0 else after)
-                send(here, here, xsend.at[j], xrecv.at[j], at.across)
-                send(here, here, csend.at[j, 0], crecv.at[j, 0], at.twin)
+                cond = holds(j, at.f)
+                arrived(here, asend.at[j], arecv.at[j], at.twin, cond)
+                send(here, here, xsend.at[j], xrecv.at[j], at.across, cond)
+                send(here, here, csend.at[j, 0], crecv.at[j, 0], at.twin, cond)
         yield
         for j in range(self.slots):
             there = o.at[j, at.f ^ 2]
-            arrived(there, xsend.at[j], xrecv.at[j], at.across)
-            send(there, there, csend.at[j, 1], crecv.at[j, 1], at.twin)
+            cond = holds(j, at.f ^ 2)
+            arrived(there, xsend.at[j], xrecv.at[j], at.across, cond)
+            send(there, there, csend.at[j, 1], crecv.at[j, 1], at.twin, cond)
             yield
         for j in range(self.slots):
             for k in range(2):
-                arrived(o.at[j, (at.f ^ 1) ^ (2 * k)], csend.at[j, k], crecv.at[j, k], at.twin)
+                other = (at.f ^ 1) ^ (2 * k)
+                arrived(o.at[j, other], csend.at[j, k], crecv.at[j, k], at.twin, holds(j, other))
         for one in sends:
             one.sent()
         own.wait()
+
+
+def runs(starts, size):
+    marks = sorted({edge for start in starts for edge in (start, start + size)})
+    found = []
+    for begin, end in zip(marks[:-1], marks[1:]):
+        found.append((begin, end, [(at, begin - start) for at, start in enumerate(starts) if start <= begin and end <= start + size]))
+    return found
+
+
+def join_kernel(terms, *refs):
+    half = len(refs) // 2
+    for term, parts_ref, out_ref in zip(terms, refs[:half], refs[half:]):
+        for begin, end, sources in term:
+            value = None
+            for at, first in sources:
+                part = parts_ref[at, :, first : first + end - begin].astype(jnp.float32)
+                value = part if value is None else value + part
+            out_ref[:, begin:end] = value
+    refs[-1][...] = refs[half - 1][0].astype(jnp.float32)
+
+
+def join(dense, dense_starts, mixer, mixer_starts, plain):
+    steps = 4
+    terms, ins, outs, shapes = [], [], [], []
+    for arrays, starts, period, every in ((dense, dense_starts, 2, 1), (mixer, mixer_starts, 4, 2)):
+        for x in arrays:
+            _, rows, size = x.shape
+            term = runs(starts[:period], size)
+            columns = term[-1][1]
+            terms.append(term)
+            ins.append(pl.BlockSpec((period, rows, size), lambda i, every=every: (i // every, 0, 0)))
+            outs.append(pl.BlockSpec((rows, columns), lambda i, every=every: (0, i // every)))
+            shapes.append(jax.ShapeDtypeStruct((rows, columns * steps // every), jnp.float32))
+    _, rows, columns = plain.shape
+    ins.append(pl.BlockSpec((1, rows, columns // steps), lambda i: (0, 0, i)))
+    outs.append(pl.BlockSpec((rows, columns // steps), lambda i: (0, i)))
+    shapes.append(jax.ShapeDtypeStruct((rows, columns), jnp.float32))
+    return pl.pallas_call(
+        functools.partial(join_kernel, terms), grid=(steps,), in_specs=ins, out_specs=outs, out_shape=shapes, name="join"
+    )(*dense, *mixer, plain)
 
 
 def rms_rows(values):
@@ -1419,7 +1534,8 @@
     letter = "m"
     reach = ("line",)
 
-    def __init__(self, x_full, w_branch, w_input, w_out, igate, dgate, gain, mask, taps, soft):
+    def __init__(self, window_of, x_full, w_branch, w_input, w_out, igate, dgate, gain, mask, taps, soft):
+        self.window_of = window_of
         _, rows, width = x_full.shape
         window, head = igate.shape
         tokens = 8 * rows
@@ -1432,6 +1548,7 @@
         self.outs += [jax.ShapeDtypeStruct(shape, kind) for shape, kind in zip(shapes, kinds)]
         self.kept = [pltpu.VMEM(shape, kind) for shape, kind in zip(shapes, kinds)]
         self.held = [pltpu.VMEM(x.shape, x.dtype) for x in self.ins[1:]]
+        self.held[2] = pltpu.VMEM((window, width), low)
         self.local = [
             pltpu.VMEM((8, rows, width), low),
             pltpu.VMEM((8 + 2 * rows, window), full),
@@ -1452,11 +1569,14 @@
         parts, padded, coef, drive, carry, lsem, ssem = take(len(self.local))
         normed, pre, conv_in, rounded, gin, gdec, states, mixed = kept
         w_branch, w_input, w_out, igate, dgate, gain, mask, taps, soft = held
-        chain = Chain(at, parts, outs[0], scratch, ascending)
+        chain = Chain(at, parts, outs[0], scratch, farthest)
         _, rows, width = normed.shape
         window, head = igate.shape
         span = 2 * rows
-        loads = [pltpu.make_async_copy(src, dst, lsem.at[i]) for i, (src, dst) in enumerate(zip(ins, [normed] + held))]
+        w_out[...] = jnp.zeros_like(w_out)
+        offset = pl.multiple_of(self.window_of.offset(at.s), 16)
+        place = lambda dst: dst.at[pl.ds(offset, ins[3].shape[0])] if dst is w_out else dst
+        loads = [pltpu.make_async_copy(src, place(dst), lsem.at[i]) for i, (src, dst) in enumerate(zip(ins, [normed] + held))]
         for load in loads:
             load.start()
         yield
@@ -1486,7 +1606,6 @@
                 padded[8:, lanes] = value.astype(jnp.float32)
             if t:
                 yield
-
             def piece(c, _):
                 for h in range(window // head):
                     lanes = slice(h * head, (h + 1) * head)
@@ -1540,10 +1659,15 @@
                 return 0
 
             lax.fori_loop(0, width // 256, product, 0)
-            chain.send_side(t)
+            if t == 0:
+                chain.send_side(0)
 
         for t in range(4):
             yield from work(t)
+            if t == 3:
+                chain.send_side(jnp.where(at.z == 3, 1, 3))
+                chain.send_side(jnp.where(at.z == 2, 1, 2))
+                chain.send_side(jnp.where(at.z == 3, 3, jnp.where(at.z == 2, 2, 1)))
             yield
         stores = [pltpu.make_async_copy(src, dst, ssem.at[i]) for i, (src, dst) in enumerate(zip(kept, outs[1:]))]
         for store in stores:
@@ -1563,7 +1687,8 @@
     letter = "b"
     reach = ("line",)
 
-    def __init__(self, out_grad, w_out, w_branch, w_input, normed, pre, conv_in, rounded, gin, gdec, states, mixed, igate, dgate, mask, ahead, taps, soft, owned):
+    def __init__(self, window_of, out_grad, w_out, w_branch, w_input, normed, pre, conv_in, rounded, gin, gdec, states, mixed, igate, dgate, mask, ahead, taps, soft, owned):
+        self.window_of = window_of
         rows, width = out_grad.shape
         tokens, window = pre.shape
         head = igate.shape[1]
@@ -1573,9 +1698,10 @@
         shape = jax.ShapeDtypeStruct
         self.outs = [
             shape((rows, width), full), shape((width, window), low), shape((width, window), low), shape((window, width), low),
-            shape((window, head), full), shape((window, head), full), shape((8, window), full),
+            shape((window, 2 * head), low), shape((window, 128), full),
         ]
         self.held = [pltpu.VMEM(x.shape, x.dtype) for x in self.ins[1:]]
+        self.held[0] = pltpu.VMEM((window, width), low)
         self.held[9] = pltpu.VMEM((8 + tokens, window), full)
         self.local = [
             pltpu.VMEM((8, rows, width), low),
@@ -1591,7 +1717,8 @@
             pltpu.VMEM((window, head), full),
             pltpu.VMEM((window, head), full),
             pltpu.VMEM((8 * 5, window), full),
-            pltpu.VMEM((8, window), full),
+            pltpu.VMEM((window, 2 * head), low),
+            pltpu.VMEM((window, 128), full),
             dma((len(self.ins),)),
             dma((8,)),
         ]
@@ -1603,7 +1730,7 @@
         scratch = list(scratch)
         take = lambda count: [scratch.pop(0) for _ in range(count)]
         held = take(len(self.held))
-        toks, parts, mgrad, pgrad, cgrad, padded, later, coef, drive, carry, igrad, dgrad, sums, lines, lsem, ssem = take(len(self.local))
+        toks, parts, mgrad, pgrad, cgrad, padded, later, coef, drive, carry, igrad, dgrad, sums, gates, lines, lsem, ssem = take(len(self.local))
         gsems = take(len(self.gather.scratch))
         w_out, w_branch, w_input, normed, pre, conv_in, rounded, gin, gdec, states, mixed, igate, dgate, mask, ahead, taps, soft, owned = held
         chain = Chain(at, parts, outs[0], scratch, descending)
@@ -1616,6 +1743,9 @@
         relay.begin()
         loads = []
         for i, (src, dst) in enumerate(zip(ins[1:], held)):
+            if dst is w_out:
+                first = pl.multiple_of(self.window_of.own - self.window_of.offset(at.s), 16)
+                src = src.at[pl.ds(first, window)]
             loads.append(pltpu.make_async_copy(src, dst.at[8:] if dst is states else dst, lsem.at[i]))
             loads[-1].start()
         states[0:8, :] = jnp.zeros((8, window), jnp.float32)
@@ -1728,14 +1858,19 @@
                 return 0
 
             lax.fori_loop(0, width // 256, product, 0)
-            chain.send_side(t)
+            if t > 1:
+                chain.send_side(t)
 
         for t in (3, 2, 1, 0):
             yield from work(t)
+            if t == 0:
+                chain.send_side(jnp.where(at.z == 0, 1, 0))
+                chain.send_side(jnp.where(at.z == 0, 0, 1))
             yield
-        for k in range(5):
-            lines[k : k + 1, :] = jnp.sum(sums[8 * k : 8 * k + 8, :], axis=0, keepdims=True)
-        lines[5:8, :] = jnp.zeros((3, window), jnp.float32)
+        gates[:, :head] = igrad[...].astype(gates.dtype)
+        gates[:, head:] = dgrad[...].astype(gates.dtype)
+        totals = [jnp.sum(sums[8 * k : 8 * k + 8, :], axis=0, keepdims=True) for k in range(5)]
+        lines[...] = jnp.concatenate(totals + [jnp.zeros((123, window), jnp.float32)], axis=0).T
 
         def grads(r):
             lanes = pl.ds(pl.multiple_of(r * 256, 256), 256)
@@ -1757,7 +1892,7 @@
         chain.finish()
         stores = [
             pltpu.make_async_copy(src, dst, ssem.at[i])
-            for i, (src, dst) in enumerate(zip((w_branch, w_input, w_out, igrad, dgrad, lines), outs[1:]))
+            for i, (src, dst) in enumerate(zip((w_branch, w_input, w_out, gates, lines), outs[1:]))
         ]
         for store in stores:
             store.start()
@@ -1797,17 +1932,13 @@
     own = width // peers
     hidden_own = gate_weight.shape[1] // peers
     all_tokens = peers * tokens
-    firsts = [min(own * at // head, width // head - 2) for at in range(peers)]
     window = 2 * head
-    offset = own * s - head * jnp.minimum(own * s // head, width // head - 2)
+    channels = Window(own, head, width, rows)
+    offset = channels.offset(s)
     owned = ((jnp.arange(window) >= offset) & (jnp.arange(window) < offset + own)).astype(jnp.float32)
 
-    small = jnp.zeros((8, 128), jnp.float32)
-    small = small.at[0, :rows].set(first_gain.astype(jnp.float32))
-    small = small.at[1, :rows].set(second_gain.astype(jnp.float32))
-    small = small.at[2, :tokens].set(resets[0].astype(jnp.float32))
-    small = jnp.broadcast_to(small[None], (peers * groups, 8, 128))
-    mixer_start = lambda to: head * jnp.minimum(own * to // head, width // head - 2)
+    wide_row = lambda v: jnp.pad(v.astype(jnp.float32), (0, 128 - v.shape[0]))
+    small = jnp.pad(jnp.stack([wide_row(first_gain), wide_row(second_gain), wide_row(resets[0])]), ((0, 5), (0, 0)))[None]
     dense_start = lambda to: 128 * (hidden_own * to // 128)
     wide = 128 * -(-hidden_own // 128)
     lanes = jnp.arange(wide) + dense_start(s) - hidden_own * s
@@ -1817,10 +1948,10 @@
     x_full, w_branch, w_input, row_w, out_w, vectors = exchange(
         [
             Gather(sources_low),
-            Spread(branch_weight, mixer_start, window),
-            Spread(input_weight, mixer_start, window),
-            Rows(row_pack, True),
-            Rows(output_weight, False),
+            Spread(branch_weight, channels.first, window),
+            Spread(input_weight, channels.first, window),
+            Rows(row_pack, channels),
+            Rows(output_weight),
             Tiny(small),
         ],
         1,
@@ -1829,15 +1960,6 @@
     whole = lambda w: w.reshape(width, w.shape[-1])
     w_branch, w_input = whole(w_branch), whole(w_input)
     w_output = out_w.reshape(own, width)
-    before = jnp.concatenate(
-        [
-            lax.ppermute(w_output[own - 192 :], "seq", [(i, i + 1) for i in range(peers - 1)]),
-            w_output,
-            lax.ppermute(w_output[:192], "seq", [(i + 1, i) for i in range(peers - 1)]),
-        ]
-    )
-    w_output_window = lax.dynamic_slice_in_dim(before, 192 - offset, window, 0)
-    w_output_own = lax.dynamic_update_slice_in_dim(jnp.zeros((window, width), low), w_output, offset, 0)
     near = lax.dynamic_slice_in_dim(row_w.reshape(3 * own, row_pack.shape[1]), own - offset, window, 0)
     w_igate, w_dgate = near[:, :head], near[:, head : 2 * head]
     taps = jnp.zeros((8, window), jnp.float32).at[:4].set(near[:, 2 * head : 2 * head + 4].astype(jnp.float32).T)
@@ -1859,16 +1981,17 @@
     gain_rows = jnp.broadcast_to(gain_first[None], (8, width))
     (
         mixer_out, normed, pre, conv_in, rounded, gate_in, gate_dec, states, mixed,
-        returned_full, w_gate, w_up, w_down,
+        returned_full, w_gate, w_up, w_down, w_output_near,
     ) = exchange(
         [
-            MixerForward(x_full, w_branch, w_input, w_output_own, w_igate, w_dgate, gain_rows, masks, taps, soft),
+            MixerForward(channels, x_full, w_branch, w_input, w_output, w_igate, w_dgate, gain_rows, masks, taps, soft),
             Gather(returned),
         ]
-        + [Spread(w, dense_start, wide) for w in (gate_weight, up_weight, down_weight)],
+        + [Spread(w, dense_start, wide) for w in (gate_weight, up_weight, down_weight)]
+        + [Rows(output_weight, channels)],
         2,
         "mixer_forward",
-        ["gs"] + [""] * 9 + ["ggggsssggggssggggsss"] + [""] * 12,
+        ["gso", "s", "", "", "s", "", "", "s", "", "", "ggggssggggssggggs"],
     )
     resid = sources + mixer_out
     scale_two = lax.rsqrt(jnp.mean(resid * resid, axis=1, keepdims=True) + EPSILON)
@@ -1886,18 +2009,19 @@
     out_grad = resid_grad.astype(low)
     split = lambda g: g.reshape(peers, groups, rows, g.shape[-1])
     (
-        normed_grad, grad_branch, grad_input, grad_output, igate_term, dgate_term, line_terms,
+        normed_grad, grad_branch, grad_input, grad_output, gates, lines,
         grad_gate, grad_up, grad_down,
     ) = exchange(
         [
             MixerBackward(
-                out_grad, w_output_window, w_branch, w_input, normed, pre, conv_in, rounded, gate_in, gate_dec, states, mixed,
+                channels, out_grad, w_output_near.reshape(3 * own, width), w_branch, w_input, normed, pre, conv_in, rounded, gate_in, gate_dec, states, mixed,
                 w_igate, w_dgate, masks, aheads, taps, soft, owned_rows,
             )
         ]
         + [Collect(split(g)) for g in (grad_gate, grad_up, grad_down)],
         4,
         "mixer_backward",
+        ["c"] * 13 + ["", "c"] * 4,
     )
     scale_one = lax.rsqrt(jnp.mean(sources * sources, axis=1, keepdims=True) + EPSILON)
     weighted = normed_grad * gain_first
@@ -1907,16 +2031,19 @@
         - sources * scale_one**3 * jnp.mean(weighted * sources, axis=1, keepdims=True)
     )
     first_term = jnp.sum(normed_grad * sources * scale_one, axis=0)
-    take_rows = lambda g: lax.dynamic_slice_in_dim(g, offset, own, 0)
-    grad_branch, grad_input, grad_output = split(grad_branch), split(grad_input), take_rows(grad_output)
-    gates = take_rows(jnp.concatenate([igate_term, dgate_term], axis=1)).astype(low)
-    lines = take_rows(jnp.concatenate([line_terms.T, jnp.zeros((window, 120), jnp.float32)], axis=1))
-    vectors = jnp.zeros((peers * groups, 8, 128), jnp.float32)
-    vectors = vectors.at[:, 0, :rows].set(first_term.reshape(peers * groups, rows))
-    vectors = vectors.at[:, 1, :rows].set(second_term.reshape(peers * groups, rows))
-    by_rows = lambda g: g.reshape(1, groups, rows, g.shape[-1])
+    grad_branch, grad_input = split(grad_branch), split(grad_input)
+    terms = jnp.stack([first_term.reshape(peers * groups, rows), second_term.reshape(peers * groups, rows)], axis=1)
+    vectors = jnp.pad(terms, ((0, 0), (0, 6), (0, 128 - rows)))
     ffn_out, grad_branch, grad_input, grad_output, gates, lines, vectors = exchange(
-        [Reduce(result_part), Collect(grad_branch), Collect(grad_input), Collect(by_rows(grad_output)), Collect(by_rows(gates)), Collect(by_rows(lines)), Tiny(vectors)],
+        [
+            Reduce(result_part),
+            Collect(grad_branch),
+            Collect(grad_input),
+            Collect(grad_output, channels),
+            Collect(gates, channels),
+            Collect(lines, channels),
+            Tiny(vectors),
+        ],
         6,
         "mixer_collect",
     )
@@ -1924,36 +2051,26 @@
     vectors = jnp.sum(vectors, axis=0)
     gates = gates[0].astype(jnp.float32)
 
-    def join(g, starts):
-        size = g.shape[-1]
-        marks = sorted({edge for start in starts for edge in (start, start + size)})
-        pieces = []
-        for low_mark, high_mark in zip(marks[:-1], marks[1:]):
-            terms = [
-                g[at, :, low_mark - start : high_mark - start].astype(jnp.float32)
-                for at, start in enumerate(starts)
-                if start <= low_mark and high_mark <= start + size
-            ]
-            pieces.append(sum(terms[1:], terms[0]))
-        return jnp.concatenate(pieces, axis=1)
-
-    firsts = [head * first for first in firsts]
-    dense_firsts = [128 * (hidden_own * at // 128) for at in range(peers)]
+    dense_grads, dense_starts = (grad_gate, grad_up, grad_down), [128 * (hidden_own * at // 128) for at in range(peers)]
+    mixer_starts = [head * min(own * at // head, width // head - 2) for at in range(peers)]
+    grad_gate, grad_up, grad_down, grad_branch, grad_input, grad_output = join(
+        dense_grads, dense_starts, (grad_branch, grad_input), mixer_starts, grad_output
+    )
     return (
         result[None],
         source_grad.astype(low)[None],
         vectors[0, :rows],
-        join(grad_branch, firsts),
-        join(grad_input, firsts),
+        grad_branch,
+        grad_input,
         lines[0, :, :4],
         gates[:, :head],
         gates[:, head:],
         lines[0, :, 4] * jax.nn.sigmoid(decay_param.astype(jnp.float32)),
-        grad_output[0].astype(jnp.float32),
+        grad_output,
         vectors[1, :rows],
-        join(grad_gate, dense_firsts),
-        join(grad_up, dense_firsts),
-        join(grad_down, dense_firsts),
+        grad_gate,
+        grad_up,
+        grad_down,
     )
 
 

time: 845 us -> 769 us (0.910)
  Pallas kernels: 763 us -> 728 us
  other arithmetic: 36.1 us -> 18.2 us
  local copies, waits for them, and re-layouts: 29.7 us -> 14.1 us
    pallas_call x5, Pallas kernels: 763 us -> 722 us  [exchange(): pl.pallas_call(kernel, out_shape=[shape for job in jobs for shape in job....]
    unnamed x51 -> x0, other arithmetic: 10.2 us -> none
  transfers between devices with their start and end apart: 2 -> 0, of which waited for: 0 -> 0; matrix products, arithmetic and copies ran while one was open for 2% -> 0% of each run, Pallas kernels for 44% -> 0%
where the time goes in v1:
time: 769 us; the launch traced here: 762 us
  Pallas kernels  728 us (95%)
  other arithmetic  18.2 us (2%)
  local copies, waits for them, and re-layouts  14.1 us (2%)
    pallas_call x5, Pallas kernels, exchange(): pl.pallas_call(kernel, out_shape=[shape for job in jobs for shape in job....  722 us

profile of v1, /device:TPU:8, one launch (start us, length us, event | category | flops | bytes accessed | tf_op | source)
XLA Modules:
  0.0 762.0 jit_solution(12708766710761181842)
XLA Ops:
  0.7 0.7 bitcast_convert_fusion.1
  1.4 0.7 convert_element_type.75
  2.0 0.6 fusion.9.refs_5_
  2.6 0.8 copy.54
  3.4 0.8 copy.55
  4.2 1.5 concatenate.23.refs_3_
  5.7 84.3 %first_exchange.1 = (bf16[8,128,2560]{2,1,0:T(8,128)(2,1)}, bf16[8,4,80,512]{3,2,1,0:T(8,128)(2,1)}, bf16[8,4,80,512]{3,2,1,0:T(8,128)(2,1)}, bf16[3,4,80,640]{3...) custom-call(bf16[128,2560]{1,0:T(8,128)(2,1)} %bitcast.66, bf16[80,2560]{1,0:T(8,128)(2,1)} %refs_1_.1, ...), custom_call_target="tpu_custom_call" | custom-call | tf_op jit(solution)/shard_map/first_exchange/pallas_call | solution.py:1397
  90.0 1.9 fusion.20
  91.9 1.0 dynamic-slice_convert_fusion
  93.0 0.1 copy.71
  93.1 0.6 broadcast_in_dim.50.refs_9_.refs_17_
  93.7 0.9 dynamic-slice.10
  94.6 0.1 copy.69
  94.7 0.6 pad_convert_fusion.refs_8_.refs_16_
  95.4 0.3 reduce-window.9
  95.7 0.1 slice.84
  95.8 0.1 slice_reduce_fusion.3
  96.0 0.1 fusion.14
  96.0 0.1 pad_maximum_fusion.1
  96.2 0.1 fusion.23
  96.3 0.6 fusion.22
  97.0 1.0 copy.60.refs_7_.refs_14_
  98.0 0.1 slice_reduce_fusion.1
  98.2 0.6 broadcast_in_dim.24.refs_6_
  98.8 205.8 %mixer_forward.1 = (f32[128,2560]{1,0:T(8,128)}, bf16[8,128,2560]{2,1,0:T(8,128)(2,1)}, f32[1024,512]{1,0:T(8,128)}, bf16[1024,512]{1,0:T(8,128)(2,1)}, bf16[102...) custom-call(bf16[8,128,2560]{2,1,0:T(8,128)(2,1)} %get-tuple-element, ...), custom_call_target="tpu_custom_call" | custom-call | tf_op jit(solution)/shard_map/mixer_forward/pallas_call | solution.py:1397
  304.6 2.2 multiply_reduce_fusion.2
  306.8 0.5 multiply_multiply_fusion.1
  307.4 1.0 multiply_convert_fusion.refs_0_
  308.4 0.6 broadcast_in_dim.51.refs_5_
  309.1 148.6 %dense.1 = (f32[128,2560]{1,0:T(8,128)}, bf16[8,128,2560]{2,1,0:T(8,128)(2,1)}, bf16[2560,1024]{1,0:T(8,128)(2,1)}, bf16[2560,1024]{1,0:T(8,128)(2,1)}, bf16[2560,1024]{1,0:T(8,128)(2,1)}) custom-call(bf16[128,2560]{1,0:T(8,128)(2,1)} %multiply_convert_fusion.refs_0_, bf16[8,128,2560]{2,1,0:T(8,128)(2,1)} %get-tuple-element.80.refs_1_, ...), custom_call_target="tpu_custom_call" | custom-call | tf_op jit(solution)/shard_map/dense/pallas_call | solution.py:1397
  457.7 1.8 multiply_reduce_fusion
  459.6 1.7 fusion.19
  461.3 0.6 broadcast_in_dim.52.refs_18_
  462.0 1.0 copy.64.refs_15_
  463.0 186.1 %mixer_backward.1 = (f32[128,2560]{1,0:T(8,128)}, bf16[2560,512]{1,0:T(8,128)(2,1)}, bf16[2560,512]{1,0:T(8,128)(2,1)}, bf16[512,2560]{1,0:T(8,128)(2,1)}, bf16[...) custom-call(bf16[128,2560]{1,0:T(8,128)(2,1)} %get-tuple-element.168, ...), custom_call_target="tpu_custom_call" | custom-call | tf_op jit(solution)/shard_map/mixer_backward/pallas_call | solution.py:1397
  649.1 1.7 fusion.6
  650.8 0.1 stack_reshape.6
  650.9 0.1 stack_reshape.7
  651.0 0.7 select_maximum_fusion.refs_6_
  651.7 96.8 %mixer_collect.1 = (f32[128,2560]{1,0:T(8,128)}, bf16[8,80,512]{2,1,0:T(8,128)(2,1)}, bf16[8,80,512]{2,1,0:T(8,128)(2,1)}, bf16[1,80,2560]{2,1,0:T(8,128)(2,1)},...) custom-call(bf16[8,128,2560]{2,1,0:T(8,128)(2,1)} %get-tuple-element.84.refs_0_, ...), custom_call_target="tpu_custom_call" | custom-call | tf_op jit(solution)/shard_map/mixer_collect/pallas_call | solution.py:1397
  748.5 6.8 join.1
  755.4 2.7 fusion.8
  758.1 1.0 fusion.7
  759.1 0.7 fusion.21
  759.8 0.7 copy.65
  760.5 0.5 slice_bitcast_fusion.1
  761.0 0.2 slice_reduce_fusion
  761.2 0.5 divide_multiply_fusion
  (55 shorter events, 0.7 us)
Async XLA Ops:
  90.0 5.3 copy-start.8
  98.8 205.8 %copy-start = (bf16[1,128,2560]{2,1,0:T(8,128)(2,1)S(1)}, bf16[1,128,2560]{2,1,0:T(8,128)(2,1)}, u32[]{:S(2)}) copy-start(bf16[1,128,2560]{2,1,0:T(8,128)(2,1)} %param.17) | copy-start | bytes 1966084
  307.3 1.1 copy-start.10
  309.1 148.6 %copy-start.11 = (f32[128]{0:T(128)S(1)}, f32[128]{0:T(128)}, u32[]{:S(2)}) copy-start(f32[128]{0:T(128)} %copy-done.10) | copy-start | bytes 1540
  457.6 1.9 copy-start.2
  457.6 1.9 copy-start.3
  457.7 1.9 copy-start.12
  457.7 1.9 copy-start.15
  459.5 2.4 copy-start.9
  463.0 186.1 %copy-start.13 = (f32[128]{0:T(128)S(1)}, f32[128]{0:T(128)}, u32[]{:S(2)}) copy-start(f32[128]{0:T(128)} %get-tuple-element.174) | copy-start | bytes 1540
  748.5 6.8 copy-start.1
  755.4 2.7 copy-start.4
  758.1 1.0 copy-start.7
  758.1 1.7 copy-start.5
  758.1 2.4 copy-start.6
  758.1 3.1 copy-start.14

commit v2 on v1

--- a/solution.py
+++ b/solution.py
@@ -1221,8 +1221,8 @@
                 put(act, value * up * keep)
                 put(ggrad, grad * up * slope * keep)
                 put(ugrad, grad * value * keep)
-                pl.when(n == 1)(lambda: relay.step(i + 2, 0))
-                pl.when(n == 3)(lambda: relay.step(i + 2, 1))
+                for p in range(PIECES // 2):
+                    pl.when(n == (p + 1) * wide // tile // (PIECES // 2) - 1)(lambda: relay.step(i + 2, p))
                 return 0
 
             lax.fori_loop(0, wide // tile, first, 0)
@@ -1235,8 +1235,8 @@
                 put = lambda ref, v: ref.__setitem__((both, slice(None), lanes), v.astype(ref.dtype).reshape(2, rows, tile))
                 put(hpart, last_dot(g, wg[lanes, :]) + last_dot(u, wu[lanes, :]))
                 put(rpart, last_dot(a, wd[lanes, :]))
-                pl.when(n == 2)(lambda: relay.step(i + 2, 2))
-                pl.when(n == 6)(lambda: relay.step(i + 2, 3))
+                for p in range(PIECES // 2):
+                    pl.when(n == 2 + p * (8 // PIECES + 1 if PIECES > 4 else 4))(lambda: relay.step(i + 2, PIECES // 2 + p))
                 return 0
 
             lax.fori_loop(0, width // tile, second, 0)
@@ -1659,15 +1659,10 @@
                 return 0
 
             lax.fori_loop(0, width // 256, product, 0)
-            if t == 0:
-                chain.send_side(0)
+            chain.send_side(t)
 
         for t in range(4):
             yield from work(t)
-            if t == 3:
-                chain.send_side(jnp.where(at.z == 3, 1, 3))
-                chain.send_side(jnp.where(at.z == 2, 1, 2))
-                chain.send_side(jnp.where(at.z == 3, 3, jnp.where(at.z == 2, 2, 1)))
             yield
         stores = [pltpu.make_async_copy(src, dst, ssem.at[i]) for i, (src, dst) in enumerate(zip(kept, outs[1:]))]
         for store in stores:
@@ -1697,7 +1692,7 @@
         self.ins = [out_grad, w_out, w_branch, w_input, normed, pre, conv_in, rounded, gin, gdec, states, mixed, igate, dgate, mask, ahead, taps, soft, owned]
         shape = jax.ShapeDtypeStruct
         self.outs = [
-            shape((rows, width), full), shape((width, window), low), shape((width, window), low), shape((window, width), low),
+            shape((rows, width), full), shape((width, window - 128), low), shape((width, window - 128), low), shape((window, width), low),
             shape((window, 2 * head), low), shape((window, 128), full),
         ]
         self.held = [pltpu.VMEM(x.shape, x.dtype) for x in self.ins[1:]]
@@ -1890,8 +1885,9 @@
             lax.fori_loop(0, PIECES, chain_step, 0)
             yield
         chain.finish()
+        owned_lanes = pl.ds(pl.multiple_of(self.window_of.offset(at.s) // 128 * 128, 128), window - 128)
         stores = [
-            pltpu.make_async_copy(src, dst, ssem.at[i])
+            pltpu.make_async_copy(src.at[:, owned_lanes] if i < 2 else src, dst, ssem.at[i])
             for i, (src, dst) in enumerate(zip((w_branch, w_input, w_out, gates, lines), outs[1:]))
         ]
         for store in stores:
@@ -1956,6 +1952,7 @@
         ],
         1,
         "first_exchange",
+        ["sot", "sso", "sso", "sso", "ss", "ss", "ss", "s", "s", "s", "s"],
     )
     whole = lambda w: w.reshape(width, w.shape[-1])
     w_branch, w_input = whole(w_branch), whole(w_input)
@@ -2021,7 +2018,7 @@
         + [Collect(split(g)) for g in (grad_gate, grad_up, grad_down)],
         4,
         "mixer_backward",
-        ["c"] * 13 + ["", "c"] * 4,
+        ["c"] * 13 + ["c", "", "c", "", "c", "", "", "c"],
     )
     scale_one = lax.rsqrt(jnp.mean(sources * sources, axis=1, keepdims=True) + EPSILON)
     weighted = normed_grad * gain_first
@@ -2046,13 +2043,14 @@
         ],
         6,
         "mixer_collect",
+        ["ct"] + ["c"] * 8 + ["", "c"] * 4 + ["c"] * 4,
     )
     result = (resid + ffn_out).astype(low)
     vectors = jnp.sum(vectors, axis=0)
     gates = gates[0].astype(jnp.float32)
 
     dense_grads, dense_starts = (grad_gate, grad_up, grad_down), [128 * (hidden_own * at // 128) for at in range(peers)]
-    mixer_starts = [head * min(own * at // head, width // head - 2) for at in range(peers)]
+    mixer_starts = [own * at // 128 * 128 for at in range(peers)]
     grad_gate, grad_up, grad_down, grad_branch, grad_input, grad_output = join(
         dense_grads, dense_starts, (grad_branch, grad_input), mixer_starts, grad_output
     )

time: 769 us -> 749 us (0.974)
  Pallas kernels: 728 us -> 711 us
    pallas_call x5, Pallas kernels: 722 us -> 704 us  [exchange(): pl.pallas_call(kernel, out_shape=[shape for job in jobs for shape in job....]
where the time goes in v2:
time: 749 us; the launch traced here: 745 us
  Pallas kernels  711 us (95%)
  other arithmetic  18.2 us (2%)
  local copies, waits for them, and re-layouts  14.1 us (2%)
    pallas_call x5, Pallas kernels, exchange(): pl.pallas_call(kernel, out_shape=[shape for job in jobs for shape in job....  704 us

profile of v2, /device:TPU:8, one launch (start us, length us, event | category | flops | bytes accessed | tf_op | source)
XLA Modules:
  0.0 744.7 jit_solution(7652206067208977535)
XLA Ops:
  0.7 0.7 bitcast_convert_fusion.1
  1.4 0.7 convert_element_type.75
  2.0 0.6 fusion.9.refs_5_
  2.6 0.8 copy.54
  3.4 0.8 copy.55
  4.2 1.5 concatenate.23.refs_3_
  5.7 82.5 %first_exchange.1 = (bf16[8,128,2560]{2,1,0:T(8,128)(2,1)}, bf16[8,4,80,512]{3,2,1,0:T(8,128)(2,1)}, bf16[8,4,80,512]{3,2,1,0:T(8,128)(2,1)}, bf16[3,4,80,640]{3...) custom-call(bf16[128,2560]{1,0:T(8,128)(2,1)} %bitcast.66, bf16[80,2560]{1,0:T(8,128)(2,1)} %refs_1_.1, ...), custom_call_target="tpu_custom_call" | custom-call | tf_op jit(solution)/shard_map/first_exchange/pallas_call | solution.py:1397
  88.2 1.9 fusion.20
  90.1 1.0 dynamic-slice_convert_fusion
  91.1 0.1 copy.71
  91.3 0.6 broadcast_in_dim.50.refs_9_.refs_17_
  91.9 0.9 dynamic-slice.10
  92.8 0.1 copy.69
  92.9 0.6 pad_convert_fusion.refs_8_.refs_16_
  93.6 0.3 reduce-window.9
  93.9 0.1 slice.84
  94.0 0.1 slice_reduce_fusion.3
  94.2 0.1 fusion.14
  94.2 0.1 pad_maximum_fusion.1
  94.4 0.1 fusion.23
  94.5 0.6 fusion.22
  95.2 1.0 copy.60.refs_7_.refs_14_
  96.2 0.1 slice_reduce_fusion.1
  96.4 0.6 broadcast_in_dim.24.refs_6_
  97.0 198.9 %mixer_forward.1 = (f32[128,2560]{1,0:T(8,128)}, bf16[8,128,2560]{2,1,0:T(8,128)(2,1)}, f32[1024,512]{1,0:T(8,128)}, bf16[1024,512]{1,0:T(8,128)(2,1)}, bf16[102...) custom-call(bf16[8,128,2560]{2,1,0:T(8,128)(2,1)} %get-tuple-element, ...), custom_call_target="tpu_custom_call" | custom-call | tf_op jit(solution)/shard_map/mixer_forward/pallas_call | solution.py:1397
  295.9 2.2 multiply_reduce_fusion.2
  298.1 0.5 multiply_multiply_fusion.1
  298.7 1.0 multiply_convert_fusion.refs_0_
  299.7 0.6 broadcast_in_dim.51.refs_5_
  300.3 152.1 %dense.1 = (f32[128,2560]{1,0:T(8,128)}, bf16[8,128,2560]{2,1,0:T(8,128)(2,1)}, bf16[2560,1024]{1,0:T(8,128)(2,1)}, bf16[2560,1024]{1,0:T(8,128)(2,1)}, bf16[2560,1024]{1,0:T(8,128)(2,1)}) custom-call(bf16[128,2560]{1,0:T(8,128)(2,1)} %multiply_convert_fusion.refs_0_, bf16[8,128,2560]{2,1,0:T(8,128)(2,1)} %get-tuple-element.80.refs_1_, ...), custom_call_target="tpu_custom_call" | custom-call | tf_op jit(solution)/shard_map/dense/pallas_call | solution.py:1397
  452.4 1.8 multiply_reduce_fusion
  454.3 1.7 fusion.19
  456.1 0.6 broadcast_in_dim.52.refs_18_
  456.7 1.0 copy.64.refs_15_
  457.7 182.9 %mixer_backward.1 = (f32[128,2560]{1,0:T(8,128)}, bf16[2560,384]{1,0:T(8,128)(2,1)}, bf16[2560,384]{1,0:T(8,128)(2,1)}, bf16[512,2560]{1,0:T(8,128)(2,1)}, bf16[...) custom-call(bf16[128,2560]{1,0:T(8,128)(2,1)} %get-tuple-element.168, ...), custom_call_target="tpu_custom_call" | custom-call | tf_op jit(solution)/shard_map/mixer_backward/pallas_call | solution.py:1397
  640.6 1.7 fusion.6
  642.3 0.1 stack_reshape.6
  642.4 0.1 stack_reshape.7
  642.5 0.7 select_maximum_fusion.refs_6_
  643.2 88.1 %mixer_collect.1 = (f32[128,2560]{1,0:T(8,128)}, bf16[8,80,384]{2,1,0:T(8,128)(2,1)}, bf16[8,80,384]{2,1,0:T(8,128)(2,1)}, bf16[1,80,2560]{2,1,0:T(8,128)(2,1)},...) custom-call(bf16[8,128,2560]{2,1,0:T(8,128)(2,1)} %get-tuple-element.84.refs_0_, ...), custom_call_target="tpu_custom_call" | custom-call | tf_op jit(solution)/shard_map/mixer_collect/pallas_call | solution.py:1397
  731.3 6.8 join.1
  738.1 2.7 fusion.8
  740.9 1.0 fusion.7
  741.9 0.7 fusion.21
  742.6 0.7 copy.65
  743.3 0.5 slice_bitcast_fusion.1
  743.8 0.2 slice_reduce_fusion
  744.0 0.5 divide_multiply_fusion
  (55 shorter events, 0.7 us)
Async XLA Ops:
  88.2 5.3 copy-start.8
  97.0 198.9 %copy-start = (bf16[1,128,2560]{2,1,0:T(8,128)(2,1)S(1)}, bf16[1,128,2560]{2,1,0:T(8,128)(2,1)}, u32[]{:S(2)}) copy-start(bf16[1,128,2560]{2,1,0:T(8,128)(2,1)} %param.17) | copy-start | bytes 1966084
  298.6 1.1 copy-start.10
  300.3 152.1 %copy-start.11 = (f32[128]{0:T(128)S(1)}, f32[128]{0:T(128)}, u32[]{:S(2)}) copy-start(f32[128]{0:T(128)} %copy-done.10) | copy-start | bytes 1540
  452.4 1.9 copy-start.2
  452.4 1.9 copy-start.3
  452.4 1.9 copy-start.12
  452.4 1.9 copy-start.15
  454.3 2.4 copy-start.9
  457.7 182.9 %copy-start.13 = (f32[128]{0:T(128)S(1)}, f32[128]{0:T(128)}, u32[]{:S(2)}) copy-start(f32[128]{0:T(128)} %get-tuple-element.174) | copy-start | bytes 1540
  731.3 6.8 copy-start.1
  738.1 2.7 copy-start.4
  740.8 1.0 copy-start.7
  740.8 1.7 copy-start.5
  740.8 2.4 copy-start.6
  740.8 3.1 copy-start.14

commit v3 on v2

--- a/solution.py
+++ b/solution.py
@@ -1163,7 +1163,7 @@
         tokens = pltpu.VMEM((8, rows, width), low)
         weight = pltpu.VMEM((width, wide), low)
         inner = pltpu.VMEM((8, rows, wide), low)
-        self.own = [tokens, tokens, weight, weight, weight, inner, inner, inner, tokens, tokens, pltpu.VMEM(held.shape, held.dtype), dma((8,))]
+        self.own = [tokens, tokens, weight, weight, weight, inner, inner, inner, tokens, tokens, pltpu.VMEM(held.shape, held.dtype), pltpu.VMEM((8 * rows, wide), jnp.float32), dma((8,))]
         self.gather = Gather(hidden)
         self.chain = Chain.scratch(rows, width, low)
         self.scratch = self.own + self.gather.scratch + self.chain
@@ -1171,7 +1171,7 @@
     def steps(self, at, ins, outs, scratch):
         hidden, returned, w_gate, w_up, w_down, held = ins
         count = len(self.own)
-        toks, cots, wg, wu, wd, act, ggrad, ugrad, hpart, rpart, mask, sems = scratch[:count]
+        toks, cots, wg, wu, wd, act, ggrad, ugrad, hpart, rpart, mask, agrad, sems = scratch[:count]
         scratch = scratch[count:]
         gsems, scratch = scratch[: len(self.gather.scratch)], scratch[len(self.gather.scratch) :]
         hchain = Chain(at, hpart, outs[0], scratch, outward)
@@ -1180,16 +1180,32 @@
         tile = 256
         loads = [
             pltpu.make_async_copy(src, dst, sems.at[i])
-            for i, (src, dst) in enumerate(((w_gate, wg), (w_up, wu), (w_down, wd), (returned, cots), (held, mask)))
+            for i, (src, dst) in enumerate(((w_down, wd), (returned, cots), (w_gate, wg), (w_up, wu), (held, mask)))
         ]
         relay = Relay(at, hidden, toks, gsems)
         relay.begin()
         for load in loads:
             load.start()
         yield
+        for load in loads[:2]:
+            load.wait()
+
+        def early(p, _):
+            source = cots[pl.ds(2 * p, 2)].reshape(2 * rows, width)
+            here = pl.ds(pl.multiple_of(2 * rows * p, 2 * rows), 2 * rows)
+
+            def one(n, _):
+                lanes = pl.ds(pl.multiple_of(n * tile, tile), tile)
+                agrad[here, lanes] = jnp.dot(source, wd[:, lanes], preferred_element_type=jnp.float32)
+                return 0
+
+            lax.fori_loop(0, wide // tile, one, 0)
+            return 0
+
         for p in range(PIECES):
+            early(p, 0)
             relay.step(1, p)
-        for load in loads:
+        for load in loads[2:]:
             load.wait()
         relay.own_copy().wait()
         last_dot = lambda a, b: lax.dot_general(a, b, CONTRACT_LAST, preferred_element_type=jnp.float32)
@@ -1211,10 +1227,9 @@
             def first(n, _):
                 lanes = pl.ds(pl.multiple_of(n * tile, tile), tile)
                 h = toks[both].reshape(2 * rows, width)
-                c = cots[both].reshape(2 * rows, width)
                 pre = jnp.dot(h, wg[:, lanes], preferred_element_type=jnp.float32)
                 up = jnp.dot(h, wu[:, lanes], preferred_element_type=jnp.float32)
-                grad = jnp.dot(c, wd[:, lanes], preferred_element_type=jnp.float32)
+                grad = agrad[pl.ds(pl.multiple_of(2 * rows * t, 2 * rows), 2 * rows), lanes]
                 value, slope = gelu_parts(pre)
                 keep = mask[0:1, lanes]
                 put = lambda ref, v: ref.__setitem__((both, slice(None), lanes), v.astype(ref.dtype).reshape(2, rows, tile))
@@ -1698,10 +1713,11 @@
         self.held = [pltpu.VMEM(x.shape, x.dtype) for x in self.ins[1:]]
         self.held[0] = pltpu.VMEM((window, width), low)
         self.held[9] = pltpu.VMEM((8 + tokens, window), full)
+        self.held[3] = pltpu.VMEM((2, 8, rows, 256), low)
         self.local = [
             pltpu.VMEM((8, rows, width), low),
             pltpu.VMEM((8, rows, width), low),
-            pltpu.VMEM((2 * rows, window), full),
+            pltpu.VMEM((tokens, window), full),
             pltpu.VMEM((tokens, window), low),
             pltpu.VMEM((tokens, window), low),
             pltpu.VMEM((2 * rows + 8, window), full),
@@ -1738,6 +1754,8 @@
         relay.begin()
         loads = []
         for i, (src, dst) in enumerate(zip(ins[1:], held)):
+            if dst is normed:
+                continue
             if dst is w_out:
                 first = pl.multiple_of(self.window_of.own - self.window_of.offset(at.s), 16)
                 src = src.at[pl.ds(first, window)]
@@ -1747,24 +1765,31 @@
         for ref in (later, carry, igrad, dgrad, sums):
             ref[...] = jnp.zeros_like(ref)
         yield
+        last_dot = lambda a, b: lax.dot_general(a, b, CONTRACT_LAST, preferred_element_type=jnp.float32)
+        far = at.z < 2
+        order = (at.z, at.z ^ 1, jnp.where(far, 2, 1), jnp.where(far, 3, 0))
+
+        def pull(t):
+            relay.wait_beside(t)
+            source = toks[pl.ds(2 * t, 2)].reshape(span, width)
+            for lanes in heads:
+                mgrad[pl.ds(pl.multiple_of(span * t, span), span), lanes] = last_dot(source, w_out[lanes, :])
+
         for d in range(1, 4):
             for p in range(PIECES):
                 relay.step(d, p)
                 yield
-        for load in loads:
-            load.wait()
-        relay.own_copy().wait()
-        for t in range(4):
-            relay.wait_beside(t)
+            if d == 1:
+                for load in loads:
+                    load.wait()
+                relay.own_copy().wait()
+            pull(order[d - 1])
+        pull(order[3])
         line = lax.broadcasted_iota(jnp.int32, (8, head), 0)
         rows_dot = lambda a, b: lax.dot_general(a, b, CONTRACT_ROWS, preferred_element_type=jnp.float32)
-        last_dot = lambda a, b: lax.dot_general(a, b, CONTRACT_LAST, preferred_element_type=jnp.float32)
         fold = lambda v: jnp.sum(v.reshape(v.shape[0] // 8, 8, v.shape[1]), axis=0)
 
         def work(t):
-            source = toks[2 * t : 2 * t + 2].reshape(span, width)
-            for lanes in heads:
-                mgrad[:, lanes] = last_dot(source, w_out[lanes, :])
             later[span : span + 8, :] = later[0:8, :]
             if t:
                 padded[0:8, :] = conv_in[span * t - 16 : span * t, :].astype(jnp.float32)[8:]
@@ -1781,7 +1806,7 @@
                 carried = 1.0 - restart
                 for lanes in heads:
                     branch, slope = gelu_parts(pre[here, lanes])
-                    grad = mgrad[inside, lanes]
+                    grad = mgrad[here, lanes]
                     state = states[pl.ds(pl.multiple_of(t * span + base, CHUNK), CHUNK + 8), lanes]
                     pgrad[here, lanes] = (grad * state[8:] * slope * owned[0:1, lanes]).astype(pgrad.dtype)
                     g_dec = gdec[here, lanes]
@@ -1867,14 +1892,20 @@
         totals = [jnp.sum(sums[8 * k : 8 * k + 8, :], axis=0, keepdims=True) for k in range(5)]
         lines[...] = jnp.concatenate(totals + [jnp.zeros((123, window), jnp.float32)], axis=0).T
 
+        def fetch(r):
+            lanes = pl.ds(pl.multiple_of(r * 256, 256), 256)
+            return pltpu.make_async_copy(ins[4].at[:, :, lanes], normed.at[lax.rem(r, 2)], ssem.at[6 + lax.rem(r, 2)])
+
         def grads(r):
             lanes = pl.ds(pl.multiple_of(r * 256, 256), 256)
-            value = normed[:, :, lanes].reshape(tokens, 256)
+            pl.when(r + 1 < width // 256)(lambda: fetch(r + 1).start())
+            fetch(r).wait()
+            value = normed[lax.rem(r, 2)].reshape(tokens, 256)
             w_branch[lanes, :] = rows_dot(value, pgrad[...]).astype(w_branch.dtype)
             w_input[lanes, :] = rows_dot(value, cgrad[...]).astype(w_input.dtype)
             w_out[:, lanes] = rows_dot(mixed[...], toks[:, :, lanes].reshape(tokens, 256)).astype(w_out.dtype)
 
-        done = 0
+        fetch(0).start()
         for k in range(3):
 
             def chain_step(p, _):

time: 749 us -> 750 us (level)
  no operation moved by 1% of the time
where the time goes in v3:
time: 750 us; the launch traced here: 746 us
  Pallas kernels  712 us (95%)
  other arithmetic  18.2 us (2%)
  local copies, waits for them, and re-layouts  14.1 us (2%)
    pallas_call x5, Pallas kernels, exchange(): pl.pallas_call(kernel, out_shape=[shape for job in jobs for shape in job....  705 us

profile of v3, /device:TPU:8, one launch (start us, length us, event | category | flops | bytes accessed | tf_op | source)
XLA Modules:
  0.0 745.8 jit_solution(17072685636071353007)
XLA Ops:
  0.7 0.7 bitcast_convert_fusion.1
  1.4 0.7 convert_element_type.75
  2.0 0.6 fusion.9.refs_5_
  2.6 0.8 copy.54
  3.4 0.8 copy.55
  4.2 1.5 concatenate.23.refs_3_
  5.7 82.5 %first_exchange.1 = (bf16[8,128,2560]{2,1,0:T(8,128)(2,1)}, bf16[8,4,80,512]{3,2,1,0:T(8,128)(2,1)}, bf16[8,4,80,512]{3,2,1,0:T(8,128)(2,1)}, bf16[3,4,80,640]{3...) custom-call(bf16[128,2560]{1,0:T(8,128)(2,1)} %bitcast.66, bf16[80,2560]{1,0:T(8,128)(2,1)} %refs_1_.1, ...), custom_call_target="tpu_custom_call" | custom-call | tf_op jit(solution)/shard_map/first_exchange/pallas_call | solution.py:1412
  88.2 1.9 fusion.20
  90.1 1.0 dynamic-slice_convert_fusion
  91.1 0.1 copy.71
  91.3 0.6 broadcast_in_dim.50.refs_9_.refs_17_
  91.9 0.9 dynamic-slice.10
  92.8 0.1 copy.69
  92.9 0.6 pad_convert_fusion.refs_8_.refs_16_
  93.6 0.3 reduce-window.9
  93.9 0.1 slice.84
  94.0 0.1 slice_reduce_fusion.3
  94.2 0.1 fusion.14
  94.2 0.1 pad_maximum_fusion.1
  94.4 0.1 fusion.23
  94.5 0.6 fusion.22
  95.2 1.0 copy.60.refs_7_.refs_14_
  96.2 0.1 slice_reduce_fusion.1
  96.4 0.6 broadcast_in_dim.24.refs_6_
  97.0 198.9 %mixer_forward.1 = (f32[128,2560]{1,0:T(8,128)}, bf16[8,128,2560]{2,1,0:T(8,128)(2,1)}, f32[1024,512]{1,0:T(8,128)}, bf16[1024,512]{1,0:T(8,128)(2,1)}, bf16[102...) custom-call(bf16[8,128,2560]{2,1,0:T(8,128)(2,1)} %get-tuple-element, ...), custom_call_target="tpu_custom_call" | custom-call | tf_op jit(solution)/shard_map/mixer_forward/pallas_call | solution.py:1412
  295.9 2.2 multiply_reduce_fusion.2
  298.1 0.5 multiply_multiply_fusion.1
  298.7 1.0 multiply_convert_fusion.refs_0_
  299.7 0.6 broadcast_in_dim.51.refs_5_
  300.3 150.7 %dense.1 = (f32[128,2560]{1,0:T(8,128)}, bf16[8,128,2560]{2,1,0:T(8,128)(2,1)}, bf16[2560,1024]{1,0:T(8,128)(2,1)}, bf16[2560,1024]{1,0:T(8,128)(2,1)}, bf16[2560,1024]{1,0:T(8,128)(2,1)}) custom-call(bf16[128,2560]{1,0:T(8,128)(2,1)} %multiply_convert_fusion.refs_0_, bf16[8,128,2560]{2,1,0:T(8,128)(2,1)} %get-tuple-element.80.refs_1_, ...), custom_call_target="tpu_custom_call" | custom-call | tf_op jit(solution)/shard_map/dense/pallas_call | solution.py:1412
  451.1 1.8 multiply_reduce_fusion
  453.0 1.7 fusion.19
  454.7 0.6 broadcast_in_dim.52.refs_18_
  455.4 1.0 copy.64.refs_15_
  456.4 181.7 %mixer_backward.1 = (f32[128,2560]{1,0:T(8,128)}, bf16[2560,384]{1,0:T(8,128)(2,1)}, bf16[2560,384]{1,0:T(8,128)(2,1)}, bf16[512,2560]{1,0:T(8,128)(2,1)}, bf16[...) custom-call(bf16[128,2560]{1,0:T(8,128)(2,1)} %get-tuple-element.168, ...), custom_call_target="tpu_custom_call" | custom-call | tf_op jit(solution)/shard_map/mixer_backward/pallas_call | solution.py:1412
  638.1 1.7 fusion.6
  639.8 0.1 stack_reshape.6
  639.9 0.1 stack_reshape.7
  640.0 0.7 select_maximum_fusion.refs_6_
  640.7 91.7 %mixer_collect.1 = (f32[128,2560]{1,0:T(8,128)}, bf16[8,80,384]{2,1,0:T(8,128)(2,1)}, bf16[8,80,384]{2,1,0:T(8,128)(2,1)}, bf16[1,80,2560]{2,1,0:T(8,128)(2,1)},...) custom-call(bf16[8,128,2560]{2,1,0:T(8,128)(2,1)} %get-tuple-element.84.refs_0_, ...), custom_call_target="tpu_custom_call" | custom-call | tf_op jit(solution)/shard_map/mixer_collect/pallas_call | solution.py:1412
  732.4 6.8 join.1
  739.2 2.7 fusion.8
  741.9 1.0 fusion.7
  742.9 0.7 fusion.21
  743.6 0.7 copy.65
  744.3 0.5 slice_bitcast_fusion.1
  744.8 0.2 slice_reduce_fusion
  745.0 0.5 divide_multiply_fusion
  (55 shorter events, 0.7 us)
Async XLA Ops:
  88.2 5.3 copy-start.8
  97.0 198.9 %copy-start = (bf16[1,128,2560]{2,1,0:T(8,128)(2,1)S(1)}, bf16[1,128,2560]{2,1,0:T(8,128)(2,1)}, u32[]{:S(2)}) copy-start(bf16[1,128,2560]{2,1,0:T(8,128)(2,1)} %param.17) | copy-start | bytes 1966084
  298.6 1.1 copy-start.10
  300.3 150.7 %copy-start.11 = (f32[128]{0:T(128)S(1)}, f32[128]{0:T(128)}, u32[]{:S(2)}) copy-start(f32[128]{0:T(128)} %copy-done.10) | copy-start | bytes 1540
  451.0 1.9 copy-start.2
  451.1 1.9 copy-start.3
  451.1 1.9 copy-start.12
  451.1 1.9 copy-start.15
  453.0 2.4 copy-start.9
  456.4 181.7 %copy-start.13 = (f32[128]{0:T(128)S(1)}, f32[128]{0:T(128)}, u32[]{:S(2)}) copy-start(f32[128]{0:T(128)} %get-tuple-element.174) | copy-start | bytes 1540
  732.4 6.8 copy-start.1
  739.2 2.7 copy-start.4
  741.9 1.0 copy-start.7
  741.9 1.7 copy-start.5
  741.9 2.4 copy-start.6
  741.9 3.1 copy-start.14
